TPU v7x, 32 devices: a whole 2x2x4 slice. The times are simulated.
32 devices in a mesh: dp: 4 (over z), ctx: 8 (over y, x, core).
Axes of the slice: x: 2, y: 2, z: 4, core: 2. Of those that a mesh axis runs over, the one named last changes fastest.
Arguments:
- inputs: bfloat16 [4, 131072, 256], P('dp', 'ctx'), may hold values from -6 to 6
- grad_out: bfloat16 [4, 131072, 256], P('dp', 'ctx'), may hold values from -6 to 6
- w_in: bfloat16 [256, 768], replicated, may hold values from -0.375 to 0.375
- filter_real: float32 [512, 512, 16], P('ctx'), may hold values from -12 to 12, as said below
- filter_imag: float32 [512, 512, 16], P('ctx'), may hold values from -12 to 12, as said below
Outputs:
- gated_out: bfloat16 [4, 131072, 256], P('dp', 'ctx')
- grad_w_in: float32 [256, 768], P('dp')
Inputs may be any that keep to these rules, and one draw needn't show every extreme that they name: Each long filter is real: with P = 262144, filter_real at frequency (P - f) mod P equals filter_real at frequency f. Each long filter is real: with P = 262144, filter_imag at frequency (P - f) mod P is minus filter_imag at frequency f.
All inputs are finite; a program needn't handle non-finite values.
Results may differ from a plain program's by a relative error of at most 0.011.
Values may be sent and summed in bfloat16 or wider, within the bound.
No kernel may reach another device: no remote copies, remote signals or barrier semaphores. Data moves between devices by JAX's collectives and lax.ppermute only.
A program may use at most 384 MiB of HBM per device.

v0:
```python
import math

import jax
import jax.numpy as jnp
from jax import lax
from jax.sharding import PartitionSpec as P

N1 = 512
N2 = 512


def dft_tables(row_index, col_index, period, factor):
    phase_angle = (row_index[:, None] * col_index[None, :] % period).astype(jnp.float32) * (
        2.0 * math.pi / period
    )
    return (
        (jnp.cos(phase_angle) * factor).astype(jnp.bfloat16),
        (jnp.sin(phase_angle) * factor).astype(jnp.bfloat16),
    )


def twiddle_tables(row_index, col_index, period):
    phase_angle = (row_index[:, None] * col_index[None, :] % period).astype(jnp.float32) * (
        2.0 * math.pi / period
    )
    return (jnp.cos(phase_angle)[:, :, None], jnp.sin(phase_angle)[:, :, None])


def combine(cos_part, sin_part, orient):
    real_part = cos_part[:, :, 0] - orient * sin_part[:, :, 1]
    imag_part = cos_part[:, :, 1] + orient * sin_part[:, :, 0]
    return (real_part, imag_part)


def rotate(real_part, imag_part, cos_table, sin_table, orient):
    new_real = real_part * cos_table - orient * imag_part * sin_table
    new_imag = imag_part * cos_table + orient * real_part * sin_table
    return (new_real, new_imag)


def pack_complex(real_part, imag_part):
    return jnp.stack([real_part, imag_part], axis=2).astype(jnp.bfloat16)


def long_conv(signal, spec_real, spec_imag, tables):
    cos_one, sin_one, cos_two, sin_two, fwd_cos, fwd_sin, inv_cos, inv_sin = tables
    block_data = lax.all_to_all(signal, "ctx", split_axis=1, concat_axis=0, tiled=True)
    cos_part = jnp.einsum("ft,tcpm->fcpm", cos_one, block_data, preferred_element_type=jnp.float32)
    sin_part = jnp.einsum("ft,tcpm->fcpm", sin_one, block_data, preferred_element_type=jnp.float32)
    real_part, imag_part = combine(cos_part, sin_part, -1.0)
    real_part, imag_part = rotate(real_part, imag_part, fwd_cos, fwd_sin, -1.0)
    spectrum = pack_complex(real_part, imag_part)
    columns = lax.all_to_all(spectrum, "ctx", split_axis=0, concat_axis=1, tiled=True)
    cos_part = jnp.einsum("fcpm,cg->fgpm", columns, cos_two, preferred_element_type=jnp.float32)
    sin_part = jnp.einsum("fcpm,cg->fgpm", columns, sin_two, preferred_element_type=jnp.float32)
    real_part, imag_part = combine(cos_part, sin_part, -1.0)
    prod_real = real_part * spec_real - imag_part * spec_imag
    prod_imag = real_part * spec_imag + imag_part * spec_real
    product = pack_complex(prod_real, prod_imag)
    cos_part = jnp.einsum("fgpm,gc->fcpm", product, cos_two, preferred_element_type=jnp.float32)
    sin_part = jnp.einsum("fgpm,gc->fcpm", product, sin_two, preferred_element_type=jnp.float32)
    real_part, imag_part = combine(cos_part, sin_part, 1.0)
    real_part, imag_part = rotate(real_part, imag_part, inv_cos, inv_sin, 1.0)
    returned = pack_complex(real_part, imag_part)
    block_data = lax.all_to_all(returned, "ctx", split_axis=1, concat_axis=0, tiled=True)
    cos_part = jnp.einsum("ft,fcpm->tcpm", cos_one, block_data, preferred_element_type=jnp.float32)
    sin_part = jnp.einsum("ft,fcpm->tcpm", sin_one, block_data, preferred_element_type=jnp.float32)
    real_part, imag_part = combine(cos_part, sin_part, 1.0)
    restored = pack_complex(real_part, imag_part)
    return lax.all_to_all(restored, "ctx", split_axis=0, concat_axis=1, tiled=True)


def per_device(inputs, grad_out, w_in, filter_real, filter_imag):
    ctx_count = lax.axis_size("ctx")
    ctx_pos = lax.axis_index("ctx")
    group_count = lax.axis_size("dp")
    tokens = inputs[0]
    cotangent = grad_out[0]
    tok_rows, chan_total = tokens.shape
    chan_half = chan_total // 2
    period = N1 * N2
    seq_len = period // 2
    row_count = N1 // ctx_count
    col_count = N2 // ctx_count
    shard_rows = tok_rows // N2
    full_index = jnp.arange(N1, dtype=jnp.int32)
    half_index = jnp.arange(N1 // 2, dtype=jnp.int32)
    second_index = jnp.arange(N2, dtype=jnp.int32)
    local_rows = ctx_pos * row_count + jnp.arange(row_count, dtype=jnp.int32)
    local_cols = ctx_pos * col_count + jnp.arange(col_count, dtype=jnp.int32)
    cos_one, sin_one = dft_tables(full_index, half_index, N1, 1.0 / math.sqrt(N1))
    cos_two, sin_two = dft_tables(second_index, second_index, N2, 1.0 / math.sqrt(N2))
    fwd_cos, fwd_sin = twiddle_tables(full_index, local_cols, period)
    inv_cos, inv_sin = twiddle_tables(local_rows, second_index, period)
    tables = (cos_one, sin_one, cos_two, sin_two, fwd_cos, fwd_sin, inv_cos, inv_sin)
    repeats = chan_half // filter_real.shape[2]
    tiled_real = jnp.tile(filter_real, (1, 1, repeats))
    tiled_imag = jnp.tile(filter_imag, (1, 1, repeats))
    features = jnp.dot(tokens, w_in, preferred_element_type=jnp.float32).astype(jnp.bfloat16)
    gate_part = features[:, :chan_total]
    key_part = features[:, chan_total : 2 * chan_total]
    value_part = features[:, 2 * chan_total :]
    mixed = (key_part.astype(jnp.float32) * value_part.astype(jnp.float32)).astype(jnp.bfloat16)
    grad_smooth = (cotangent.astype(jnp.float32) * gate_part.astype(jnp.float32)).astype(
        jnp.bfloat16
    )
    mixed_grid = mixed.reshape(shard_rows, N2, 2, chan_half)
    grad_grid = grad_smooth.reshape(shard_rows, N2, 2, chan_half)
    smooth_grid = long_conv(mixed_grid, tiled_real, tiled_imag, tables)
    back_grid = long_conv(grad_grid, tiled_real, -tiled_imag, tables)
    smooth = smooth_grid.reshape(tok_rows, chan_total).astype(jnp.float32)
    gated = (gate_part.astype(jnp.float32) * smooth).astype(jnp.bfloat16)
    grad_gate = (cotangent.astype(jnp.float32) * smooth).astype(jnp.bfloat16)
    grad_mixed = back_grid.reshape(tok_rows, chan_total).astype(jnp.float32)
    grad_key = (grad_mixed * value_part.astype(jnp.float32)).astype(jnp.bfloat16)
    grad_value = (grad_mixed * key_part.astype(jnp.float32)).astype(jnp.bfloat16)
    grad_features = jnp.concatenate([grad_gate, grad_key, grad_value], axis=1)
    scale = 1.0 / math.sqrt(inputs.shape[0] * group_count * seq_len)
    share_rows = chan_total // group_count
    full_term = lax.dot_general(
        tokens, grad_features, (((0,), (0,)), ((), ())), preferred_element_type=jnp.float32
    )
    everything = lax.psum(full_term, ("dp", "ctx"))
    summed = lax.dynamic_slice_in_dim(everything, lax.axis_index("dp") * share_rows, share_rows, 0)
    return (gated[None], summed * scale)


def solution(mesh):
    placed = (
        P("dp", "ctx", None),
        P("dp", "ctx", None),
        P(),
        P("ctx", None, None),
        P("ctx", None, None),
    )
    return jax.shard_map(
        per_device,
        mesh=mesh,
        in_specs=placed,
        out_specs=(P("dp", "ctx", None), P("dp", None)),
        check_vma=False,
    )
```

profile of v0, /device:TPU:0, one launch (start us, length us, event | category | flops | bytes accessed | tf_op | source)
XLA Modules:
  0.0 1950.3 jit_solution(8702917198255136217)
XLA Ops:
  19.2 22.7 %convolution_convert_fusion = bf16[16384,768]{0,1:T(8,128)(2,1)} fusion(bf16[256,768]{1,0:T(8,128)(2,1)S(1)} %copy-done, bf16[1,16384,256]{2,1,0:T(8,128)(2,1)} %param.5), kind=kOutput, calls=%fused_computation | convolution fusion | flops 6455033856 | bytes 33947648 | tf_op jit(solution)/shard_map/dot_general | solution.py:99
  41.8 14.5 fusion.11
  66.7 16.0 copy.70
  98.6 15.9 copy.52
  114.5 68.1 %all-to-all-done.4 = bf16[32,512,2,128]{3,2,0,1:T(2,128)(2,1)} async-done(((bf16[32,512,2,128]{3,2,0,1:T(2,128)(2,1)}), bf16[32,512,2,128]{3,2,0,1:T(2,128)(2,1)}, u32[]{:S(2)}, u32[]{:S(2)}) %all-to-all-start.4) | async-done | bytes 8388640 | tf_op jit(solution)/shard_map/all_to_all | solution.py:47
  188.2 16.4 copy.71
  204.6 12.5 copy.72
  217.1 17.6 fusion.56
  234.7 14.3 fusion.64
  249.0 32.6 %all-to-all-done = bf16[32,512,2,128]{3,2,0,1:T(2,128)(2,1)} async-done(((bf16[32,512,2,128]{3,2,0,1:T(2,128)(2,1)}), bf16[32,512,2,128]{3,2,0,1:T(2,128)(2,1)}, u32[]{:S(2)}, u32[]{:S(2)}) %all-to-all-start) | async-done | bytes 8388640 | tf_op jit(solution)/shard_map/all_to_all | solution.py:47
  281.6 16.3 copy.53
  298.0 12.5 copy.54
  310.5 17.6 fusion.62
  328.1 14.1 fusion.66
  342.1 49.8 %subtract_convert_fusion.2 = (bf16[512,64,1,128]{3,0,2,1:T(8,128)(2,1)}, bf16[512,64,1,128]{3,0,2,1:T(8,128)(2,1)}, bf16[512,64,1,128]{3,0,2,1:T(8,128)(2,1)S(1)}, bf16[512,64,1,128]{3,0,2,1:T(8,128)(2,1)}) fusion(f32[512,64]{0,1:T(8,128)S(1)} %get-tuple-element.37, f32[512,64]{0,1:T(8,128)S(1)} %get-tuple-element.36, f32[512,64,2,128]{3,0,2,1:T(8,128)} %fusion.56, ...), kind=kLoop, calls=%fused_computation.52 | loop fusion | flops 100663296 | bytes 168034304 | tf_op jit(solution)/shard_map/convert.13
  398.2 40.4 %copy.57 = bf16[512,64,2,128]{3,2,1,0:T(2,128)(2,1)} copy(bf16[512,64,2,128]{3,0,2,1:T(8,128)(2,1)S(1)} %pad_maximum_fusion) | data formatting | bytes 33554432 | tf_op jit(solution)/shard_map/stack | solution.py:42
  452.3 40.2 %copy.75 = bf16[512,64,2,128]{3,2,1,0:T(2,128)(2,1)} copy(bf16[512,64,2,128]{3,0,2,1:T(8,128)(2,1)S(1)} %pad_maximum_fusion.3) | data formatting | bytes 33554432 | tf_op jit(solution)/shard_map/stack | solution.py:42
  492.5 135.7 %all-to-all-done.1 = bf16[512,64,2,128]{3,2,1,0:T(2,128)(2,1)} async-done(((bf16[512,64,2,128]{3,2,1,0:T(2,128)(2,1)}), bf16[512,64,2,128]{3,2,1,0:T(2,128)(2,1)}, u32[]{:S(2)}, u32[]{:S(2)}) %all-to-all-start.1) | async-done | bytes 16777248 | tf_op jit(solution)/shard_map/all_to_all | solution.py:53
  642.0 17.6 copy.59
  667.6 17.4 copy.60
  686.3 15.2 copy.58
  701.5 24.2 %convolution_bitcast_fusion.6 = f32[64,512,2,128]{3,1,2,0:T(8,128)} fusion(bf16[64,512,2,128]{3,1,2,0:T(8,128)(2,1)} %bitcast.136), kind=kOutput, calls=%fused_computation.65 | convolution fusion | flops 8594128896 | bytes 50331648 | tf_op jit(solution)/shard_map/fcpm,cg->fgpm/dot_general | solution.py:55
  725.8 24.5 %convolution_bitcast_fusion.7 = f32[64,512,2,128]{3,1,2,0:T(8,128)} fusion(bf16[64,512,2,128]{3,1,2,0:T(8,128)(2,1)} %bitcast.137), kind=kOutput, calls=%fused_computation.66 | convolution fusion | flops 8594128896 | bytes 50331648 | tf_op jit(solution)/shard_map/fcpm,cg->fgpm/dot_general | solution.py:54
  750.3 67.7 %all-to-all-done.5 = bf16[512,64,2,128]{3,2,1,0:T(2,128)(2,1)} async-done(((bf16[512,64,2,128]{3,2,1,0:T(2,128)(2,1)}), bf16[512,64,2,128]{3,2,1,0:T(2,128)(2,1)}, u32[]{:S(2)}, u32[]{:S(2)}) %all-to-all-start.5) | async-done | bytes 16777248 | tf_op jit(solution)/shard_map/all_to_all | solution.py:53
  818.0 15.2 copy.76
  833.2 24.2 %convolution_bitcast_fusion.2 = f32[64,512,2,128]{3,1,2,0:T(8,128)} fusion(bf16[64,512,2,128]{3,1,2,0:T(8,128)(2,1)} %bitcast.138), kind=kOutput, calls=%fused_computation.61 | convolution fusion | flops 8594128896 | bytes 50331648 | tf_op jit(solution)/shard_map/fcpm,cg->fgpm/dot_general | solution.py:55
  857.4 24.6 %convolution_bitcast_fusion.3 = f32[64,512,2,128]{3,1,2,0:T(8,128)} fusion(bf16[64,512,2,128]{3,1,2,0:T(8,128)(2,1)} %bitcast.139), kind=kOutput, calls=%fused_computation.62 | convolution fusion | flops 8594128896 | bytes 50331648 | tf_op jit(solution)/shard_map/fcpm,cg->fgpm/dot_general | solution.py:54
  882.0 64.1 %subtract_convert_fusion.1 = (bf16[64,512,1,128]{3,1,2,0:T(8,128)(2,1)}, bf16[64,512,1,128]{3,1,2,0:T(8,128)(2,1)}, bf16[64,512,1,128]{3,1,2,0:T(8,128)(2,1)}, bf16[64,512,1,128]{3,1,2,0:T(8,128)(2,1)}) fusion(f32[64,512,1,128]{3,1,2,0:T(8,128)} %copy.59, f32[64,512,1,128]{3,1,2,0:T(8,128)} %copy.60, f32[64,512,2,128]{3,1,2,0:T(8,128)} %convolution_bitcast_fusion.2, ...), kind=kLoop, calls=%fused_computation.50 | loop fusion | flops 104857600 | bytes 201326592 | tf_op jit(solution)/shard_map/convert.11
  946.1 25.7 %convolution_bitcast_fusion.5 = f32[64,512,2,128]{3,1,2,0:T(8,128)} fusion(bf16[64,512,1,128]{3,1,2,0:T(8,128)(2,1)} %get-tuple-element.24, bf16[64,512,1,128]{3,1,2,0:T(8,128)(2,1)} %get-tuple-element.25), kind=kOutput, calls=%fused_computation.64 | convolution fusion | flops 8627683328 | bytes 50331648 | tf_op jit(solution)/shard_map/fgpm,gc->fcpm/dot_general | solution.py:60
  971.8 25.8 %convolution_bitcast_fusion.4 = f32[64,512,2,128]{3,1,2,0:T(8,128)} fusion(bf16[64,512,1,128]{3,1,2,0:T(8,128)(2,1)} %get-tuple-element.24, bf16[64,512,1,128]{3,1,2,0:T(8,128)(2,1)} %get-tuple-element.25), kind=kOutput, calls=%fused_computation.63 | convolution fusion | flops 8627683328 | bytes 50331648 | tf_op jit(solution)/shard_map/fgpm,gc->fcpm/dot_general | solution.py:61
  997.5 25.7 %convolution_bitcast_fusion.1 = f32[64,512,2,128]{3,1,2,0:T(8,128)} fusion(bf16[64,512,1,128]{3,1,2,0:T(8,128)(2,1)} %get-tuple-element.9, bf16[64,512,1,128]{3,1,2,0:T(8,128)(2,1)} %get-tuple-element.8), kind=kOutput, calls=%fused_computation.60 | convolution fusion | flops 8627683328 | bytes 50331648 | tf_op jit(solution)/shard_map/fgpm,gc->fcpm/dot_general | solution.py:60
  1023.2 26.1 %convolution_bitcast_fusion = f32[64,512,2,128]{3,1,2,0:T(8,128)} fusion(bf16[64,512,1,128]{3,1,2,0:T(8,128)(2,1)} %get-tuple-element.9, bf16[64,512,1,128]{3,1,2,0:T(8,128)(2,1)} %get-tuple-element.8), kind=kOutput, calls=%fused_computation.59 | convolution fusion | flops 8627683328 | bytes 50331648 | tf_op jit(solution)/shard_map/fgpm,gc->fcpm/dot_general | solution.py:61
  1049.3 54.3 %subtract_convert_fusion = (bf16[64,512,1,128]{3,1,2,0:T(8,128)(2,1)}, bf16[64,512,1,128]{3,1,2,0:T(8,128)(2,1)}, bf16[64,512,1,128]{3,1,2,0:T(8,128)(2,1)}, bf16[64,512,1,128]{3,1,2,0:T(8,128)(2,1)}) fusion(f32[64,512]{1,0:T(8,128)S(1)} %copy-done.8, f32[64,512]{1,0:T(8,128)S(1)} %copy-done.7, f32[64,512,2,128]{3,1,2,0:T(8,128)} %convolution_bitcast_fusion, ...), kind=kLoop, calls=%fused_computation.48 | loop fusion | flops 83886080 | bytes 168034304 | tf_op jit(solution)/shard_map/convert.9
  1111.7 40.2 %copy.63 = bf16[64,512,2,128]{3,2,0,1:T(2,128)(2,1)} copy(bf16[64,512,2,128]{3,1,2,0:T(8,128)(2,1)S(1)} %pad_maximum_fusion.2) | data formatting | bytes 33554432 | tf_op jit(solution)/shard_map/stack | solution.py:42
  1165.8 40.2 %copy.80 = bf16[64,512,2,128]{3,2,0,1:T(2,128)(2,1)} copy(bf16[64,512,2,128]{3,1,2,0:T(8,128)(2,1)S(1)} %pad_maximum_fusion.5) | data formatting | bytes 33554432 | tf_op jit(solution)/shard_map/stack | solution.py:42
  1206.0 135.7 %all-to-all-done.2 = bf16[64,512,2,128]{3,2,0,1:T(2,128)(2,1)} async-done(((bf16[64,512,2,128]{3,2,0,1:T(2,128)(2,1)}), bf16[64,512,2,128]{3,2,0,1:T(2,128)(2,1)}, u32[]{:S(2)}, u32[]{:S(2)}) %all-to-all-start.2) | async-done | bytes 16777248 | tf_op jit(solution)/shard_map/all_to_all | solution.py:65
  1376.9 14.5 fusion.24
  1397.6 13.2 copy.65
  1410.8 120.6 %all-to-all-done.6 = bf16[64,512,2,128]{3,2,0,1:T(2,128)(2,1)} async-done(((bf16[64,512,2,128]{3,2,0,1:T(2,128)(2,1)}), bf16[64,512,2,128]{3,2,0,1:T(2,128)(2,1)}, u32[]{:S(2)}, u32[]{:S(2)}) %all-to-all-start.6) | async-done | bytes 16777248 | tf_op jit(solution)/shard_map/all_to_all | solution.py:65
  1565.9 14.5 fusion.22
  1586.7 13.2 copy.82
  1599.9 30.8 %all-to-all-done.3 = bf16[256,64,2,128]{3,2,1,0:T(2,128)(2,1)} async-done(((bf16[256,64,2,128]{3,2,1,0:T(2,128)(2,1)}), bf16[256,64,2,128]{3,2,1,0:T(2,128)(2,1)}, u32[]{:S(2)}, u32[]{:S(2)}) %all-to-all-start.3) | async-done | bytes 8388640 | tf_op jit(solution)/shard_map/all_to_all | solution.py:70
  1652.5 17.4 copy.67
  1669.9 59.7 %all-to-all-done.7 = bf16[256,64,2,128]{3,2,1,0:T(2,128)(2,1)} async-done(((bf16[256,64,2,128]{3,2,1,0:T(2,128)(2,1)}), bf16[256,64,2,128]{3,2,1,0:T(2,128)(2,1)}, u32[]{:S(2)}, u32[]{:S(2)}) %all-to-all-start.7) | async-done | bytes 8388640 | tf_op jit(solution)/shard_map/all_to_all | solution.py:70
  1746.3 17.4 copy.84
  1763.7 33.6 %fusion.9 = (bf16[16384,256]{0,1:T(8,128)(2,1)}, bf16[16384,256]{0,1:T(8,128)(2,1)}, bf16[1,16384,256]{1,2,0:T(8,128)(2,1)}, bf16[16384,256]{0,1:T(8,128)(2,1)}) fusion(f32[16384,256]{0,1:T(8,128)} %copy.84, bf16[16384,768]{0,1:T(8,128)(2,1)} %convolution_convert_fusion, f32[16384,256]{0,1:T(8,128)} %copy.67, bf16[1,16384,256]{1,2,0:T(8,128)(2,1)} %copy.68), kind=kLoop, calls=%fused_computation.16 | loop fusion | flops 50331648 | bytes 100663296 | tf_op jit(solution)/shard_map/convert_element_type | solution.py:115
  1797.3 14.3 fusion.27
  1823.6 117.5 %all-reduce.2.cloned.1.call-done = f32[256,768]{0,1:T(8,128)} async-done(((f32[256,768]{0,1:T(8,128)}), f32[256,768]{0,1:T(8,128)}) %all-reduce.2.cloned.1.call-update) | async-done | bytes 786448 | tf_op jit(solution)/shard_map/psum | solution.py:123
  (59 shorter events, 243.7 us)
Async XLA Ops:
  7.2 12.0 copy-start
  19.1 22.7 %copy-start.4 = (bf16[1,16384,256]{1,2,0:T(8,128)(2,1)S(1)}, bf16[1,16384,256]{1,2,0:T(8,128)(2,1)}, u32[]{:S(2)}) copy-start(bf16[1,16384,256]{1,2,0:T(8,128)(2,1)} %copy.68) | copy-start | bytes 25165828
  82.7 99.9 %all-to-all-start.4 = ((bf16[32,512,2,128]{3,2,0,1:T(2,128)(2,1)}), bf16[32,512,2,128]{3,2,0,1:T(2,128)(2,1)}, u32[]{:S(2)}, u32[]{:S(2)}) async-start(bf16[32,512,2,128]{3,2,0,1:T(2,128)(2,1)} %copy.70), calls=%async_computation.4 | async-start | bytes 16777216 | tf_op jit(solution)/shard_map/all_to_all | solution.py:47
  182.6 99.0 %all-to-all-start = ((bf16[32,512,2,128]{3,2,0,1:T(2,128)(2,1)}), bf16[32,512,2,128]{3,2,0,1:T(2,128)(2,1)}, u32[]{:S(2)}, u32[]{:S(2)}) async-start(bf16[32,512,2,128]{3,2,0,1:T(2,128)(2,1)} %copy.52), calls=%async_computation | async-start | bytes 16777216 | tf_op jit(solution)/shard_map/all_to_all | solution.py:47
  187.6 29.5 %copy-start.9 = (s32[64]{0:T(128)}, s32[64]{0:T(128)S(1)}, u32[]{:S(2)}) copy-start(s32[64]{0:T(128)S(1)} %iota_add_fusion) | copy-start | bytes 772
  217.1 17.6 copy-start.2
  310.5 17.6 copy-start.3
  438.6 189.7 %all-to-all-start.1 = ((bf16[512,64,2,128]{3,2,1,0:T(2,128)(2,1)}), bf16[512,64,2,128]{3,2,1,0:T(2,128)(2,1)}, u32[]{:S(2)}, u32[]{:S(2)}) async-start(bf16[512,64,2,128]{3,2,1,0:T(2,128)(2,1)} %copy.57), calls=%async_computation.1 | async-start | bytes 33554432 | tf_op jit(solution)/shard_map/all_to_all | solution.py:53
  492.5 141.5 %copy-start.5 = (f32[64,512,16]{1,2,0:T(8,128)S(1)}, f32[64,512,16]{1,2,0:T(8,128)}, u32[]{:S(2)}) copy-start(f32[64,512,16]{1,2,0:T(8,128)} %param.8) | copy-start | bytes 6291460
  628.2 189.7 %all-to-all-start.5 = ((bf16[512,64,2,128]{3,2,1,0:T(2,128)(2,1)}), bf16[512,64,2,128]{3,2,1,0:T(2,128)(2,1)}, u32[]{:S(2)}, u32[]{:S(2)}) async-start(bf16[512,64,2,128]{3,2,1,0:T(2,128)(2,1)} %copy.75), calls=%async_computation.5 | async-start | bytes 33554432 | tf_op jit(solution)/shard_map/all_to_all | solution.py:53
  642.0 17.6 copy-start.6
  667.6 17.4 copy-start.10
  1023.2 26.1 %copy-start.7 = (f32[64,512]{1,0:T(8,128)S(1)}, f32[64,512]{1,0:T(8,128)}, u32[]{:S(2)}) copy-start(f32[64,512]{1,0:T(8,128)} %get-tuple-element.38) | copy-start | bytes 393220
  1023.2 26.1 %copy-start.8 = (f32[64,512]{1,0:T(8,128)S(1)}, f32[64,512]{1,0:T(8,128)}, u32[]{:S(2)}) copy-start(f32[64,512]{1,0:T(8,128)} %get-tuple-element.39) | copy-start | bytes 393220
  1151.8 189.8 %all-to-all-start.2 = ((bf16[64,512,2,128]{3,2,0,1:T(2,128)(2,1)}), bf16[64,512,2,128]{3,2,0,1:T(2,128)(2,1)}, u32[]{:S(2)}, u32[]{:S(2)}) async-start(bf16[64,512,2,128]{3,2,0,1:T(2,128)(2,1)} %copy.63), calls=%async_computation.2 | async-start | bytes 33554432 | tf_op jit(solution)/shard_map/all_to_all | solution.py:65
  1341.7 189.7 %all-to-all-start.6 = ((bf16[64,512,2,128]{3,2,0,1:T(2,128)(2,1)}), bf16[64,512,2,128]{3,2,0,1:T(2,128)(2,1)}, u32[]{:S(2)}, u32[]{:S(2)}) async-start(bf16[64,512,2,128]{3,2,0,1:T(2,128)(2,1)} %copy.80), calls=%async_computation.6 | async-start | bytes 33554432 | tf_op jit(solution)/shard_map/all_to_all | solution.py:65
  1531.4 99.2 %all-to-all-start.3 = ((bf16[256,64,2,128]{3,2,1,0:T(2,128)(2,1)}), bf16[256,64,2,128]{3,2,1,0:T(2,128)(2,1)}, u32[]{:S(2)}, u32[]{:S(2)}) async-start(bf16[256,64,2,128]{3,2,1,0:T(2,128)(2,1)} %copy.65), calls=%async_computation.3 | async-start | bytes 16777216 | tf_op jit(solution)/shard_map/all_to_all | solution.py:70
  1630.6 99.0 %all-to-all-start.7 = ((bf16[256,64,2,128]{3,2,1,0:T(2,128)(2,1)}), bf16[256,64,2,128]{3,2,1,0:T(2,128)(2,1)}, u32[]{:S(2)}, u32[]{:S(2)}) async-start(bf16[256,64,2,128]{3,2,1,0:T(2,128)(2,1)} %copy.82), calls=%async_computation.7 | async-start | bytes 16777216 | tf_op jit(solution)/shard_map/all_to_all | solution.py:70
  1635.6 305.4 %all-reduce.2.cloned.1.call-start = ((), (), s32[]{:S(2)}) async-start(), calls=%async_computation.8 | async-start | bytes 1572864 | tf_op jit(solution)/shard_map/psum | solution.py:123
  1797.3 145.7 %copy-start.1 = (bf16[256,768]{1,0:T(8,128)(2,1)S(1)}, bf16[256,768]{1,0:T(8,128)(2,1)}, u32[]{:S(2)}) copy-start(bf16[256,768]{1,0:T(8,128)(2,1)} %param.7) | copy-start | bytes 1179652
Sparse Core Ops, SparseCore 0:
  1811.8 129.2 all-reduce.1
where the time goes:
time: 1960 us; the launch traced here: 1950 us
  waiting for transfers between devices  768 us (39%)
  local copies, waits for them, and re-layouts  492 us (25%)
  matrix products  341 us (17%)
  other arithmetic  291 us (15%)
  starting transfers between devices  43.7 us (2%)
    all_to_all x2, waiting for transfers between devices, long_conv(): lax.all_to_all(returned, 'ctx', split_axis=1, concat_axis=0, tiled=True)  256 us
    all_to_all x2, waiting for transfers between devices, long_conv(): lax.all_to_all(spectrum, 'ctx', split_axis=0, concat_axis=1, tiled=True)  203 us
    another operation x5, other arithmetic  197 us
    another operation x6, local copies, waits for them, and re-layouts, pack_complex(): return jnp.stack([real_part, imag_part], axis=2).astype(jnp.bfloat16)  187 us
    psum x1, waiting for transfers between devices, per_device(): everything = lax.psum(full_term, ('dp', 'ctx'))  117 us
    all_to_all x2, waiting for transfers between devices, long_conv(): lax.all_to_all(signal, 'ctx', split_axis=1, concat_axis=0, tiled=True)  101 us
    all_to_all x2, waiting for transfers between devices, long_conv(): lax.all_to_all(restored, 'ctx', split_axis=0, concat_axis=1, tiled=True)  90.5 us
    unnamed x29, local copies, waits for them, and re-layouts  62.1 us
  transfers between devices with their start and end apart: 9, of which 9 were waited for; matrix products, arithmetic and copies ran while one was open for 24% of the time, Pallas kernels for 0%

commit v1 on v0

v1 whole, which is shorter than its diff:
```python
import functools
import math

import jax
import jax.numpy as jnp
import ml_dtypes
import numpy as np
from jax import lax
from jax.experimental import pallas as pl
from jax.experimental.pallas import tpu as pltpu
from jax.sharding import PartitionSpec as P

BF = jnp.bfloat16
F32 = jnp.float32
VMEM_BYTES = 60 * 1024 * 1024
POS_SPEC = pl.BlockSpec(memory_space=pltpu.SMEM)


def dot_nn(left, right):
    return lax.dot_general(left, right, (((1,), (0,)), ((), ())), preferred_element_type=F32)


def dot_nt(left, right):
    return lax.dot_general(left, right, (((1,), (1,)), ((), ())), preferred_element_type=F32)


def dot_tn(left, right):
    return lax.dot_general(left, right, (((0,), (0,)), ((), ())), preferred_element_type=F32)


def rounded(value):
    return value.astype(BF).astype(F32)


def transform_tables(n_one, n_two):
    def table(rows, cols, period):
        angle = (np.arange(rows)[:, None] * np.arange(cols)[None, :] % period) * (
            2.0 * math.pi / period
        )
        factor = 1.0 / math.sqrt(period)
        return (
            (np.cos(angle) * factor).astype(np.float32).astype(ml_dtypes.bfloat16),
            (np.sin(angle) * factor).astype(np.float32).astype(ml_dtypes.bfloat16),
        )

    cos_one, sin_one = table(n_one, n_one // 2, n_one)
    cos_two, sin_two = table(n_two, n_two, n_two)
    period = n_one * n_two
    angle = (np.arange(n_one)[:, None] * np.arange(n_two)[None, :] % period) * (
        2.0 * math.pi / period
    )
    first = np.block([[cos_one, sin_one], [-sin_one, cos_one]])
    second = np.block([[cos_two, -sin_two], [sin_two, cos_two]])
    third = np.block([[cos_two, sin_two], [-sin_two, cos_two]])
    fourth = np.block([[cos_one.T, -sin_one.T], [sin_one.T, cos_one.T]])
    return (
        first,
        second,
        third,
        fourth,
        np.cos(angle).astype(np.float32),
        np.sin(angle).astype(np.float32),
    )


def channel_order(chan_half, filters, ctx_count, chunks):
    repeats = chan_half // filters
    per_device = chan_half // ctx_count
    per_chunk = per_device // chunks
    order = []
    for chunk in range(chunks):
        for device in range(ctx_count):
            for part in range(2):
                for place in range(per_chunk):
                    index = device * per_device + chunk * per_chunk + place
                    group, repeat = divmod(index, repeats)
                    order.append(part * chan_half + repeat * filters + group)
    return np.array(order)


def gather_rows(pos_ref, pick_ref, held_ref, peers, blocks, rows):
    pos = pos_ref[0]
    chunks = pick_ref.shape[0] // (peers * rows)
    spot = 0
    for block in blocks:
        for chunk in range(chunks):
            start = pl.multiple_of((chunk * peers + (pos ^ block)) * rows, rows)
            held_ref[spot : spot + rows, :] = pick_ref[pl.ds(start, rows), :]
            spot += rows


def key_value_weights(w_ref, held_ref, wt_ref):
    count, chan = held_ref.shape
    for part in range(2):
        block = w_ref[:, (1 + part) * chan : (2 + part) * chan]
        wt_ref[part * count : (part + 1) * count, :] = dot_nt(held_ref[...], block).astype(BF)


def store_blocks(value, outs, step):
    chunks, _, rows, _ = outs[0].shape
    spot = 0
    for out in outs:
        for chunk in range(chunks):
            out[chunk, step] = value[spot : spot + rows]
            spot += rows


def load_blocks(parts, step):
    chunks = parts[0].shape[0]
    return jnp.concatenate(
        [part[chunk, step] for part in parts for chunk in range(chunks)], axis=0
    ).astype(F32)


def mixed_kernel(pos_ref, tok_ref, w_ref, pick_ref, *rest, peers, blocks):
    outs, (held_ref, wt_ref) = rest[:-2], rest[-2:]
    _, steps, rows, width = outs[0].shape
    count = held_ref.shape[0]

    @pl.when(pl.program_id(0) == 0)
    def _():
        gather_rows(pos_ref, pick_ref, held_ref, peers, blocks, rows)
        key_value_weights(w_ref, held_ref, wt_ref)

    for step in range(steps):
        feats = rounded(dot_nt(wt_ref[...], tok_ref[step * width : (step + 1) * width, :]))
        store_blocks((feats[:count] * feats[count:]).astype(BF), outs, step)


def grad_kernel(pos_ref, tok_ref, cot_ref, w_ref, pick_ref, *rest, peers):
    outs, (held_ref, wt_ref) = rest[:-2], rest[-2:]
    _, steps, rows, width = outs[0].shape
    chan = pick_ref.shape[1]

    @pl.when(pl.program_id(0) == 0)
    def _():
        gather_rows(pos_ref, pick_ref, held_ref, peers, range(peers), rows)
        wt_ref[...] = dot_nt(held_ref[...], w_ref[:, :chan]).astype(BF)

    for step in range(steps):
        span = slice(step * width, (step + 1) * width)
        gate = rounded(dot_nt(wt_ref[...], tok_ref[span, :]))
        cot = dot_nt(held_ref[...], cot_ref[span, :])
        store_blocks((gate * cot).astype(BF), outs, step)


def convolve(signal, refs, filt_real, filt_imag, orient, hold_ref):
    first_ref, second_ref, third_ref, fourth_ref, cos_ref, sin_ref = refs
    n_one = cos_ref.shape[0]
    n_two = cos_ref.shape[1]
    block = n_one // 2
    for start in range(0, n_one, block):
        span = slice(start, start + block)
        low = slice(n_one + start, n_one + start + block)
        cos, sin = cos_ref[span, :], sin_ref[span, :]
        real = dot_nn(first_ref[span, :], signal)
        imag = dot_nn(first_ref[low, :], signal)
        turned = jnp.concatenate(
            [(real * cos + imag * sin).astype(BF), (imag * cos - real * sin).astype(BF)], axis=1
        )
        spec = dot_nn(turned, second_ref[...])
        real, imag = spec[:, :n_two], spec[:, n_two:]
        f_real = filt_real(span).astype(F32)
        f_imag = filt_imag(span).astype(F32) * orient
        product = jnp.concatenate(
            [
                (real * f_real - imag * f_imag).astype(BF),
                (real * f_imag + imag * f_real).astype(BF),
            ],
            axis=1,
        )
        back = dot_nn(product, third_ref[...])
        real, imag = back[:, :n_two], back[:, n_two:]
        hold_ref[span, :] = (real * cos - imag * sin).astype(BF)
        hold_ref[low, :] = (imag * cos + real * sin).astype(BF)
    return dot_nn(fourth_ref[...], hold_ref[...])


def conv_kernel(pos_ref, *args, peers, rows, orient):
    ins, rest = args[:peers], args[peers:]
    tables, rest = rest[:6], rest[6:]
    parts_ref, rest = rest[0], rest[1:]
    outs, (in_ref, res_ref, hold_ref, filt_ref) = rest[-4 - peers : -4], rest[-4:]
    lanes = 128
    _, size, width = ins[0].shape
    times = peers * size // rows
    half = rows // 2
    place = pl.program_id(0)
    pos = pos_ref[0]
    piece = math.gcd(size, 256)

    @pl.when(place == 0)
    def _():
        groups, _, _, _, quarter, _ = parts_ref.shape
        for block in range(peers):
            base = (pos ^ block) * size
            for group in range(groups):
                start = (block * groups + group) * quarter
                span = slice(start, start + quarter)
                for part in range(2):
                    filt_ref[part, span, :] = parts_ref[group, block, 0, part]

            @pl.loop(0, size // piece)
            def _(index):
                wide = ins[block][0, pl.ds(pl.multiple_of(index * piece, piece), piece), :]
                wide = wide.astype(F32)
                span = pl.ds(pl.multiple_of(base + index * piece, piece), piece)
                for lane in range(width // lanes):
                    in_ref[lane, span, :] = wide[:, lane * lanes : (lane + 1) * lanes]

    parts = []
    for part in range(2):
        columns = [
            in_ref[lane, pl.ds(place + part * half, times, stride=rows), :].astype(BF)
            for lane in range(width // lanes)
        ]
        parts.append(jnp.concatenate(columns, axis=1))
    signal = jnp.concatenate(parts, axis=0)
    result = convolve(
        signal,
        tables,
        lambda span: filt_ref[0, span, :],
        lambda span: filt_ref[1, span, :],
        orient,
        hold_ref,
    )
    for part in range(2):
        for lane in range(width // lanes):
            res_ref[lane, pl.ds(place + part * half, times, stride=rows), :] = result[
                part * times : (part + 1) * times, lane * lanes : (lane + 1) * lanes
            ]

    @pl.when(place == pl.num_programs(0) - 1)
    def _():
        for block in range(peers):
            base = (pos ^ block) * size

            @pl.loop(0, size // piece)
            def _(index):
                span = pl.ds(pl.multiple_of(base + index * piece, piece), piece)
                outs[block][0, pl.ds(pl.multiple_of(index * piece, piece), piece), :] = (
                    jnp.concatenate(
                        [res_ref[lane, span, :] for lane in range(width // lanes)], axis=1
                    ).astype(BF)
                )


def conv_plain_kernel(x_ref, first, second, third, fourth, cos, sin, fr_ref, fi_ref, out_ref,
                      hold_ref, *, orient):
    out_ref[0] = convolve(
        x_ref[0],
        (first, second, third, fourth, cos, sin),
        lambda span: fr_ref[0, span, :],
        lambda span: fi_ref[0, span, :],
        orient,
        hold_ref,
    ).astype(BF)


def whole(shape):
    zeros = (0,) * len(shape)
    return pl.BlockSpec(shape, lambda *_: zeros, pipeline_mode=pl.Buffered(1))


def params():
    return pltpu.CompilerParams(
        dimension_semantics=("arbitrary",), vmem_limit_bytes=VMEM_BYTES
    )


def conv_cost(count, n_one, n_two, moved):
    macs = count * 2 * (n_one * n_one * n_two + 2 * n_one * n_two * n_two)
    return pl.CostEstimate(flops=2 * macs, bytes_accessed=moved, transcendentals=0)


def run_conv(blocks, tables, parts, chunk, repeats, orient, pos, joined):
    peers = len(blocks)
    chunks, size, width = blocks[0].shape
    n_one, n_two = tables[4].shape
    rows = size * peers // (n_one // 2)
    half = rows // 2
    table_specs = [whole(table.shape) for table in tables]
    block_spec = pl.BlockSpec(
        (1, size, width), lambda place: (chunk, 0, 0), pipeline_mode=pl.Buffered(1)
    )
    parts_shape = parts.shape[:2] + (1,) + parts.shape[3:]
    place_of = (0, 0, chunk * half // repeats, 0, 0, 0)
    parts_spec = pl.BlockSpec(
        parts_shape, lambda place: place_of, pipeline_mode=pl.Buffered(1)
    )
    moved = 4 * peers * size * width
    moved += sum(table.size * table.dtype.itemsize for table in tables)
    slots = pltpu.VMEM((width // 128, peers * size, 128), F32)
    first = 1 + peers + len(tables) + 1
    out_spec = pl.BlockSpec((1, size, width), lambda place: (chunk, 0, 0))
    return list(pl.pallas_call(
        functools.partial(conv_kernel, peers=peers, rows=rows, orient=orient),
        grid=(half,),
        in_specs=[POS_SPEC] + [block_spec] * peers + table_specs + [parts_spec]
        + [pl.BlockSpec(memory_space=pl.ANY)] * len(joined),
        out_specs=[out_spec] * peers,
        out_shape=[jax.ShapeDtypeStruct((chunks, size, width), BF)] * peers,
        input_output_aliases={first + index: index for index in range(len(joined))},
        scratch_shapes=[
            slots, slots, pltpu.VMEM((2 * n_one, n_two), BF), pltpu.VMEM((2, n_one, n_two), BF)
        ],
        compiler_params=params(),
        cost_estimate=conv_cost(half, n_one, n_two, moved),
        name="conv",
    )(pos, *blocks, *tables, parts, *joined))


def run_conv_plain(blocks, tables, filt, repeats, orient):
    sources, shard_rows, rows, width = blocks.shape
    n_one, n_two = tables[4].shape
    times = sources * shard_rows
    half = rows // 2
    filters = filt[0].shape[0]
    filt_spec = pl.BlockSpec(
        (1, n_one, n_two), lambda place: (jnp.minimum(place // repeats, filters - 1), 0, 0)
    )
    moved = 4 * blocks.size
    signal = blocks.reshape(times, 2, half, width).transpose(2, 1, 0, 3)
    signal = signal.reshape(half, 2 * times, width)
    channel_spec = pl.BlockSpec((1, 2 * times, width), lambda place: (place, 0, 0))
    result = pl.pallas_call(
        functools.partial(conv_plain_kernel, orient=orient),
        grid=(half,),
        in_specs=[channel_spec] + [whole(table.shape) for table in tables] + [filt_spec] * 2,
        out_specs=channel_spec,
        out_shape=jax.ShapeDtypeStruct(signal.shape, BF),
        scratch_shapes=[pltpu.VMEM((2 * n_one, n_two), BF)],
        compiler_params=params(),
        cost_estimate=conv_cost(half, n_one, n_two, moved),
        name="conv_plain",
    )(signal, *tables, *filt)
    result = result.reshape(half, 2, times, width).transpose(2, 1, 0, 3)
    return result.reshape(blocks.shape)


def store_sum(pos_ref, total, sum_ref, turn_ref, peers, blocks, chunks, rows):
    pos = pos_ref[0]
    kinds = total.shape[0] // (len(blocks) * chunks * rows)
    spot = 0
    if len(blocks) < peers:
        turn_ref[...] = jnp.zeros_like(turn_ref)
    for kind in range(kinds):
        for block in blocks:
            for chunk in range(chunks):
                start = ((kind * chunks + chunk) * peers + (pos ^ block)) * rows
                span = pl.ds(pl.multiple_of(start, rows), rows)
                turn_ref[span, :] = total[spot : spot + rows]
                spot += rows
    sum_ref[...] = turn_ref[...].T


def smooth_kernel(pos_ref, tok_ref, cot_ref, w_ref, pick_ref, *rest):
    parts, (gated_ref, sum_ref, held_ref, wt_ref, total_ref, turn_ref) = rest[:-6], rest[-6:]
    chunks, steps, rows, width = parts[0].shape
    peers = len(parts)
    chan = pick_ref.shape[1]

    @pl.when(pl.program_id(0) == 0)
    def _():
        gather_rows(pos_ref, pick_ref, held_ref, peers, range(peers), rows)
        wt_ref[...] = dot_nt(held_ref[...], w_ref[:, :chan]).astype(BF)
        total_ref[...] = jnp.zeros_like(total_ref)

    total = total_ref[...]
    for step in range(steps):
        span = slice(step * width, (step + 1) * width)
        tokens = tok_ref[span, :]
        gate = rounded(dot_nt(wt_ref[...], tokens))
        cot = dot_nt(held_ref[...], cot_ref[span, :])
        smooth = load_blocks(parts, step)
        gated_ref[span, :] = dot_tn((gate * smooth).astype(BF), held_ref[...]).astype(BF)
        total = total + dot_nn((cot * smooth).astype(BF), tokens)
    total_ref[...] = total

    @pl.when(pl.program_id(0) == pl.num_programs(0) - 1)
    def _():
        store_sum(pos_ref, total, sum_ref, turn_ref, peers, range(peers), chunks, rows)


def back_kernel(pos_ref, tok_ref, w_ref, pick_ref, *rest, peers, blocks):
    parts, rest = rest[: len(blocks)], rest[len(blocks) :]
    earlier, (sum_ref, held_ref, wt_ref, total_ref, turn_ref) = rest[:-5], rest[-5:]
    chunks, steps, rows, width = parts[0].shape
    count = len(blocks) * chunks * rows

    @pl.when(pl.program_id(0) == 0)
    def _():
        gather_rows(pos_ref, pick_ref, held_ref, peers, blocks, rows)
        key_value_weights(w_ref, held_ref, wt_ref)
        total_ref[...] = jnp.zeros_like(total_ref)

    total = total_ref[...]
    for step in range(steps):
        tokens = tok_ref[step * width : (step + 1) * width, :]
        feats = rounded(dot_nt(wt_ref[...], tokens))
        mixed = load_blocks(parts, step)
        grads = jnp.concatenate(
            [(mixed * feats[count:]).astype(BF), (mixed * feats[:count]).astype(BF)], axis=0
        )
        total = total + dot_nn(grads, tokens)
    total_ref[...] = total

    @pl.when(pl.program_id(0) == pl.num_programs(0) - 1)
    def _():
        store_sum(pos_ref, total, sum_ref, turn_ref, peers, blocks, chunks, rows)
        for ref in earlier:
            sum_ref[...] += ref[...]


def halves(peers):
    order = [block for block in range(2, peers, 2)] + [block for block in range(3, peers, 2)]
    return tuple(order[: peers // 2 - 1]), tuple(order[peers // 2 - 1 :] + [1, 0])


def send(blocks, group):
    arrived = list(blocks)
    peers = len(blocks)
    for block in group:
        if block:
            pairs = [(device, device ^ block) for device in range(peers)]
            arrived[block] = lax.ppermute(blocks[block], "ctx", pairs)
    return arrived


def exchange(blocks):
    return lax.all_to_all(blocks, "ctx", split_axis=0, concat_axis=0, tiled=True)


def own_filters(filter_real, filter_imag, ctx_count, group_count, group_pos):
    rows, n_two, filters = filter_real.shape
    quarter = rows // group_count
    own = lax.dynamic_slice_in_dim(
        jnp.stack([filter_real, filter_imag]), group_pos * quarter, quarter, 1
    )
    own = own.astype(BF).transpose(3, 0, 1, 2)
    if ctx_count > filters:
        own = jnp.repeat(own, ctx_count // filters, axis=0)
    return own.reshape(ctx_count, own.shape[0] // ctx_count, 2, quarter, n_two)


def gather_filters(own):
    return lax.all_gather(exchange(own), "dp", axis=0, tiled=False)


def after(first, value):
    return lax.optimization_barrier((value, first))


def reduce_groups(value):
    count = lax.axis_size("dp")
    pos = lax.axis_index("dp")
    split = value.reshape(count, value.shape[0] // count, value.shape[1])
    total = lax.dynamic_index_in_dim(split, pos, 0, keepdims=False)
    for step in range(1, count):
        pairs = [(device, (device + step) % count) for device in range(count)]
        sent = lax.dynamic_index_in_dim(split, (pos + step) % count, 0, keepdims=False)
        total = total + lax.ppermute(sent, "dp", pairs)
    return total


def reduce_tokens(value):
    count = lax.axis_size("ctx")
    step = 1
    while step < count:
        pairs = [(device, device ^ step) for device in range(count)]
        value = value + lax.ppermute(value, "ctx", pairs)
        step *= 2
    return value


def with_kernels(arrays, tables, pick, chunks, repeats, group_pos):
    tokens, cotangent, w_in, filter_real, filter_imag = arrays
    peers = lax.axis_size("ctx")
    tok_rows, chan = tokens.shape
    width = tables[4].shape[1]
    shard_rows = tok_rows // width
    rows = chan // (peers * chunks)
    count = peers * rows
    me = lax.axis_index("ctx").astype(jnp.int32)
    pos = me.reshape(1)
    steps = math.gcd(shard_rows, 4)
    grid = (shard_rows // steps,)
    tok_spec = pl.BlockSpec((steps * width, chan), lambda i: (i, 0))
    part_spec = pl.BlockSpec((chunks, steps, rows, width), lambda i: (0, i, 0, 0))
    chunk_spec = pl.BlockSpec((1, steps, rows, width), lambda i: (0, i, 0, 0))
    part_out = jax.ShapeDtypeStruct((chunks, shard_rows, rows, width), BF)
    w_spec, pick_spec = whole(w_in.shape), whole(pick.shape)
    macs = tok_rows * chan * chan

    def held(count, kind=BF):
        return pltpu.VMEM((count, chan), kind)

    def cost(times, moved):
        return pl.CostEstimate(
            flops=int(2 * macs * times), bytes_accessed=int(moved * 2 * tok_rows * chan),
            transcendentals=0,
        )

    def conv(blocks, chunk, orient, last, joined):
        return run_conv(blocks, tables, parts, chunk, repeats, orient, last, joined)

    def shaped(blocks, shape):
        return [block.reshape(shape) for block in blocks]

    early, late = halves(peers)
    first_group, second_group = early + late[:1], late[1:]
    flat = (chunks, shard_rows * rows, width)

    mixed = [None] * peers
    last = pos
    for group in (first_group, second_group):
        some = len(group) * chunks * rows
        outs = pl.pallas_call(
            functools.partial(mixed_kernel, peers=peers, blocks=group),
            grid=grid,
            in_specs=[POS_SPEC, tok_spec, w_spec, pick_spec],
            out_specs=[part_spec] * len(group),
            out_shape=[part_out] * len(group),
            scratch_shapes=[held(some), held(2 * some)],
            compiler_params=params(),
            cost_estimate=cost(1, 1.5),
            name="mixed",
        )(last, tokens, w_in, pick)
        last, outs = after(list(outs), pos)
        for block, out in zip(group, outs):
            mixed[block] = out
    own = own_filters(filter_real, filter_imag, peers, lax.axis_size("dp"), group_pos)
    own, mixed[0] = after(mixed[0], own)
    mine = exchange(own)
    arrived = send(send(mixed, first_group), second_group)
    (last, mine), held_back = after([arrived[block] for block in early], (last, mine))
    for block, value in zip(early, held_back):
        arrived[block] = value
    grads = list(pl.pallas_call(
        functools.partial(grad_kernel, peers=peers),
        grid=grid,
        in_specs=[POS_SPEC, tok_spec, tok_spec, w_spec, pick_spec],
        out_specs=[part_spec] * peers,
        out_shape=[part_out] * peers,
        scratch_shapes=[held(chan), held(chan)],
        compiler_params=params(),
        cost_estimate=cost(2, 3),
        name="grad_smooth",
    )(last, tokens, cotangent, w_in, pick))
    parts = lax.all_gather(mine, "dp", axis=0, tiled=False)

    arrived = shaped(arrived, flat)
    grads = shaped(grads, flat)
    joined = conv(arrived, 0, 1.0, pos, [])
    grads = send(grads, early)
    (last, grads), joined = after(joined, (pos, grads))
    joined = conv(arrived, 1, 1.0, last, joined)
    grads = send(grads, late)
    last, joined = after(joined, pos)
    back = conv(grads, 0, -1.0, last, [])
    smooth = send(joined, early)
    (last, smooth), back = after(back, (pos, smooth))
    back = conv(grads, 1, -1.0, last, back)
    smooth = send(smooth, late)
    last, back = after(back, pos)
    back = send(back, early)

    gated, gate_sum = pl.pallas_call(
        smooth_kernel,
        grid=grid,
        in_specs=[POS_SPEC, tok_spec, tok_spec, w_spec, pick_spec] + [part_spec] * peers,
        out_specs=[tok_spec, pl.BlockSpec((chan, chan), lambda i: (0, 0))],
        out_shape=[
            jax.ShapeDtypeStruct((tok_rows, chan), BF), jax.ShapeDtypeStruct((chan, chan), F32)
        ],
        scratch_shapes=[held(chan), held(chan), held(chan, F32), held(chan, F32)],
        compiler_params=params(),
        cost_estimate=cost(4, 4),
        name="smooth",
    )(last, tokens, cotangent, w_in, pick, *shaped(smooth, part_out.shape))
    (last, back), gate_sum = after(gate_sum, (pos, back))
    back = send(back, late)
    sum_shape = (chan, 2 * chan)
    back_sum = []
    for group in (early, late):
        some = len(group) * chunks * rows
        blocks = shaped([back[block] for block in group], part_out.shape)
        back_sum = [pl.pallas_call(
            functools.partial(back_kernel, peers=peers, blocks=group),
            grid=grid,
            in_specs=[POS_SPEC, tok_spec, w_spec, pick_spec] + [part_spec] * len(group)
            + [whole(sum_shape)] * len(back_sum),
            out_specs=pl.BlockSpec(sum_shape, lambda i: (0, 0)),
            out_shape=jax.ShapeDtypeStruct(sum_shape, F32),
            scratch_shapes=[
                held(some), held(2 * some), held(2 * some, F32), held(2 * chan, F32)
            ],
            compiler_params=params(),
            cost_estimate=cost(2, 2),
            name="back",
        )(last, tokens, w_in, pick, *blocks, *back_sum)]
        if group == early:
            gate_sum, back_sum = after(back_sum, gate_sum)
            gate_sum = reduce_tokens(reduce_groups(gate_sum))
            last, gate_sum = after(gate_sum, pos)
    return gated, gate_sum, reduce_tokens(reduce_groups(back_sum[0]))


def without_kernels(arrays, tables, pick, rows, repeats, group_pos):
    tokens, cotangent, w_in, filter_real, filter_imag = arrays
    peers = lax.axis_size("ctx")
    tok_rows, chan = tokens.shape
    width = tables[4].shape[1]
    shard_rows = tok_rows // width
    wt = [
        dot_nt(pick, w_in[:, part * chan : (part + 1) * chan]).astype(BF) for part in range(3)
    ]
    gate, key, value = [dot_nt(block, tokens).astype(BF).astype(F32) for block in wt]
    cot = dot_nt(pick, cotangent)
    own = own_filters(filter_real, filter_imag, peers, lax.axis_size("dp"), group_pos)
    parts = gather_filters(own)
    groups, _, each, _, quarter, _ = parts.shape
    filt = parts.transpose(3, 2, 1, 0, 4, 5).reshape(2, each, peers * groups * quarter, width)

    def convolved(array, orient):
        array = array.astype(BF).reshape(peers, rows, shard_rows, width).transpose(0, 2, 1, 3)
        result = run_conv_plain(exchange(array), tables, (filt[0], filt[1]), repeats, orient)
        result = exchange(result).transpose(0, 2, 1, 3)
        return result.reshape(chan, tok_rows).astype(F32)

    smooth = convolved(key * value, 1.0)
    back = convolved(gate * cot, -1.0)
    gated = dot_tn((gate * smooth).astype(BF), pick).astype(BF)
    terms = [cot * smooth, back * value, back * key]
    sums = [dot_nn(term.astype(BF), tokens).T for term in terms]
    summed = reduce_tokens(reduce_groups(jnp.concatenate(sums, axis=1)))
    return gated, summed[:, :chan], summed[:, chan:]


def per_device(inputs, grad_out, w_in, filter_real, filter_imag):
    ctx_count = lax.axis_size("ctx")
    group_count = lax.axis_size("dp")
    tokens = inputs[0]
    cotangent = grad_out[0]
    tok_rows, chan_total = tokens.shape
    chan_half = chan_total // 2
    n_one = filter_real.shape[0] * ctx_count
    n_two = filter_real.shape[1]
    filters = filter_real.shape[2]
    repeats = chan_half // filters
    seq_len = n_one * n_two // 2
    shard_rows = tok_rows // n_two
    per_device_chan = chan_half // ctx_count
    quarter = filter_real.shape[0] // group_count
    use_kernels = (
        per_device_chan % 16 == 0 and quarter % 16 == 0 and repeats % (per_device_chan // 2) == 0
        and ctx_count & (ctx_count - 1) == 0
    )
    chunks = 2 if use_kernels else 1
    rows = 2 * (per_device_chan // chunks)

    tables = tuple(jnp.asarray(table) for table in transform_tables(n_one, n_two))
    order = channel_order(chan_half, filters, ctx_count, chunks)
    pick_np = np.zeros((chan_total, chan_total), np.float32)
    pick_np[np.arange(chan_total), order] = 1.0
    pick = jnp.asarray(pick_np.astype(ml_dtypes.bfloat16))
    group_pos = lax.axis_index("dp")
    arrays = (tokens, cotangent, w_in, filter_real, filter_imag)
    if use_kernels:
        gated, gate_sum, back_sum = with_kernels(
            arrays, tables, pick, chunks, repeats, group_pos
        )
    else:
        gated, gate_sum, back_sum = without_kernels(
            arrays, tables, pick, rows, repeats, group_pos
        )

    scale = 1.0 / math.sqrt(inputs.shape[0] * group_count * seq_len)

    summed = jnp.concatenate([gate_sum, back_sum], axis=1)
    ordered = jnp.dot(
        summed.reshape(-1, chan_total), pick.astype(F32), precision=lax.Precision.HIGHEST
    )
    summed = ordered.reshape(summed.shape)
    return (gated[None], summed * scale)


def solution(mesh):
    placed = (
        P("dp", "ctx", None),
        P("dp", "ctx", None),
        P(),
        P("ctx", None, None),
        P("ctx", None, None),
    )
    return jax.shard_map(
        per_device,
        mesh=mesh,
        in_specs=placed,
        out_specs=(P("dp", "ctx", None), P("dp", None)),
        check_vma=False,
    )
```

time: 1960 us -> 485 us (0.25)
  waiting for transfers between devices: 768 us -> 102 us
  local copies, waits for them, and re-layouts: 492 us -> 4.17 us
  matrix products: 341 us -> 0.24 us
  other arithmetic: 291 us -> 2.17 us
  Pallas kernels: 0 us -> 276 us
  blocking collectives: 0 us -> 40.7 us
    all_to_all x8 -> x0, waiting for transfers between devices: 651 us -> none  [the longest x2 256 us: long_conv(): lax.all_to_all(returned, 'ctx', split_axis=1, concat_axis=0, tiled=True)]
    dot_general x18 -> x1, matrix products: 341 us -> 0.24 us  [per_device(): jnp.dot(summed.reshape(-1, chan_total), pick.astype(F32), precision=lax.P...]
    pallas_call x0 -> x10, Pallas kernels: none -> 276 us  [the longest x4 200 us: run_conv(): pl.pallas_call(functools.partial(conv_kernel, peers=peers, rows=rows, ori...]
    another operation x11 -> x0, other arithmetic: 240 us -> none
    another operation x10 -> x0, local copies, waits for them, and re-layouts: 238 us -> none  [the longest x6 187 us: pack_complex(): return jnp.stack([real_part, imag_part], axis=2).astype(jnp.bfloat16)]
    psum x1 -> x0, waiting for transfers between devices: 117 us -> none  [per_device(): everything = lax.psum(full_term, ('dp', 'ctx'))]
    all_to_all x8 -> x0, local copies, waits for them, and re-layouts: 108 us -> none  [the longest x4 57.7 us: long_conv(): lax.all_to_all(signal, 'ctx', split_axis=1, concat_axis=0, tiled=True)]
    ppermute x0 -> x40, waiting for transfers between devices: none -> 102 us  [the longest x28 54.5 us: send(): arrived[block] = lax.ppermute(blocks[block], 'ctx', pairs)]
  transfers between devices with their start and end apart: 9 -> 41, of which waited for: 9 -> 14; matrix products, arithmetic and copies ran while one was open for 24% -> 0% of each run, Pallas kernels for 0% -> 52%
where the time goes in v1:
time: 485 us; the launch traced here: 483 us
  Pallas kernels  276 us (57%)
  waiting for transfers between devices  102 us (21%)
  starting transfers between devices  43.9 us (9%)
  blocking collectives  40.7 us (8%)
  between operations  14.4 us (3%)
    pallas_call x4, Pallas kernels, run_conv(): pl.pallas_call(functools.partial(conv_kernel, peers=peers, rows=rows, ori...  200 us
    ppermute x28, waiting for transfers between devices, send(): arrived[block] = lax.ppermute(blocks[block], 'ctx', pairs)  54.5 us
    all_to_all x1, blocking collectives, exchange(): lax.all_to_all(blocks, 'ctx', split_axis=0, concat_axis=0, tiled=True)  40.7 us
    ppermute x6, waiting for transfers between devices, reduce_tokens(): value = value + lax.ppermute(value, 'ctx', pairs)  29.4 us
    ppermute x28, starting transfers between devices, send(): arrived[block] = lax.ppermute(blocks[block], 'ctx', pairs)  29.2 us
    pallas_call x2, Pallas kernels, with_kernels(): pl.pallas_call(functools.partial(back_kernel, peers=peers, blocks=group),...  24.5 us
    pallas_call x1, Pallas kernels, with_kernels(): pl.pallas_call(smooth_kernel, grid=grid, in_specs=[POS_SPEC, tok_spec, to...  18.9 us
    pallas_call x2, Pallas kernels, with_kernels(): pl.pallas_call(functools.partial(mixed_kernel, peers=peers, blocks=group)...  18.7 us
  transfers between devices with their start and end apart: 41, of which 14 were waited for; matrix products, arithmetic and copies ran while one was open for 0% of the time, Pallas kernels for 52%

profile of v1, /device:TPU:0, one launch (start us, length us, event | category | flops | bytes accessed | tf_op | source)
XLA Modules:
  0.0 483.3 jit_solution(10901913306228813242)
XLA Ops:
  7.2 9.4 %mixed.2 = (bf16[2,32,16,512]{3,2,1,0:T(8,128)(2,1)}, bf16[2,32,16,512]{3,2,1,0:T(8,128)(2,1)}, bf16[2,32,16,512]{3,2,1,0:T(8,128)(2,1)}, bf16[2,32,16,512]{3,2,1,0:T(8,128)(2,1)}) custom-call(s32[1]{0:T(128)} %bitcast.pos_ref, bf16[16384,256]{1,0:T(8,128)(2,1)} %bitcast.70, bf16[256,768]{1,0:T(8,128)(2,1)} %w_ref.11, bf16[256,256]{1,0:T(8,128)(2,1)} %constant.87.clone.pick_ref), custom_call_target="tpu_custom_call" | custom-call | flops 2147483648 | bytes 12582912 | tf_op jit(solution)/shard_map/mixed/pallas_call | solution.py:518
  16.6 3.0 collective-permute-start
  19.6 1.5 collective-permute-start.1
  21.1 9.3 %mixed.3 = (bf16[2,32,16,512]{3,2,1,0:T(8,128)(2,1)}, bf16[2,32,16,512]{3,2,1,0:T(8,128)(2,1)}, bf16[2,32,16,512]{3,2,1,0:T(8,128)(2,1)}, bf16[2,32,16,512]{3,2,1,0:T(8,128)(2,1)}) custom-call(s32[1]{0:T(128)} %bitcast.pos_ref, bf16[16384,256]{1,0:T(8,128)(2,1)} %bitcast.71, bf16[256,768]{1,0:T(8,128)(2,1)} %w_ref.11, bf16[256,256]{1,0:T(8,128)(2,1)} %constant.87.clone.pick_ref), custom_call_target="tpu_custom_call" | custom-call | flops 2147483648 | bytes 12582912 | tf_op jit(solution)/shard_map/mixed/pallas_call | solution.py:518
  31.9 40.7 %all_to_all.5 = bf16[8,2,2,16,512]{4,3,2,1,0:T(8,128)(2,1)} all-to-all(bf16[8,2,2,16,512]{4,3,2,1,0:T(8,128)(2,1)S(1)} %bitcast.80), channel_id=1, replica_groups=mesh['dp'=4,'ctx'=8] {'ctx'}, dimensions={0} | all-to-all | bytes 1048576 | tf_op jit(solution)/shard_map/all_to_all | solution.py:431
  72.7 1.6 collective-permute-start.8
  74.9 1.1 collective-permute-start.7
  76.1 13.7 %grad_smooth.1 = (bf16[2,32,16,512]{3,2,1,0:T(8,128)(2,1)}, bf16[2,32,16,512]{3,2,1,0:T(8,128)(2,1)}, bf16[2,32,16,512]{3,2,1,0:T(8,128)(2,1)}, bf16[2,32,16,512...) custom-call(s32[1]{0:T(128)} %bitcast.pos_ref, ...), custom_call_target="tpu_custom_call" | custom-call | flops 4294967296 | bytes 25165824 | tf_op jit(solution)/shard_map/grad_smooth/pallas_call | solution.py:539
  91.7 1.1 collective-permute-start.4
  92.9 27.8 %collective-permute-done.8 = bf16[2,32,16,512]{3,2,1,0:T(8,128)(2,1)S(1)} collective-permute-done((bf16[2,32,16,512]{3,2,1,0:T(8,128)(2,1)}, bf16[2,32,16,512]{3,2,1,0:T(8,128)(2,1)S(1)}, u32[]{:S(2)}, u32[]{:S(2)}) %collective-permute-start.8) | collective-permute-done | bytes 1048608 | tf_op jit(solution)/shard_map/ppermute | solution.py:426
  121.6 1.2 collective-permute-start.5
  122.9 49.9 %conv.4 = (bf16[2,512,512]{2,1,0:T(8,128)(2,1)}, bf16[2,512,512]{2,1,0:T(8,128)(2,1)}, bf16[2,512,512]{2,1,0:T(8,128)(2,1)}, bf16[2,512,512]{2,1,0:T(8,128)(2,1)...) custom-call(s32[1]{0:T(128)} %bitcast.pos_ref, ...), custom_call_target="tpu_custom_call" | custom-call | flops 12884901888 | bytes 16777216 | tf_op jit(solution)/shard_map/conv/pallas_call | solution.py:296
  172.8 1.2 collective-permute-start.13
  173.9 1.2 collective-permute-start.14
  175.7 1.2 collective-permute-start.16
  176.8 49.9 %conv.5 = (bf16[2,512,512]{2,1,0:T(8,128)(2,1)}, bf16[2,512,512]{2,1,0:T(8,128)(2,1)}, bf16[2,512,512]{2,1,0:T(8,128)(2,1)}, bf16[2,512,512]{2,1,0:T(8,128)(2,1)...) custom-call(s32[1]{0:T(128)} %bitcast.pos_ref, ...), custom_call_target="tpu_custom_call", output_to_operand_aliasing={{0}: (16, {}), {1}: (17, {}), {2}: (18, {}), {3}: (19, {}),... | custom-call | flops 12884901888 | bytes 16777216 | tf_op jit(solution)/shard_map/conv/pallas_call | solution.py:296
  226.7 1.6 collective-permute-start.10
  228.8 1.5 collective-permute-start.12
  230.3 50.2 %conv.6 = (bf16[2,512,512]{2,1,0:T(8,128)(2,1)}, bf16[2,512,512]{2,1,0:T(8,128)(2,1)}, bf16[2,512,512]{2,1,0:T(8,128)(2,1)}, bf16[2,512,512]{2,1,0:T(8,128)(2,1)...) custom-call(s32[1]{0:T(128)} %bitcast.pos_ref, ...), custom_call_target="tpu_custom_call" | custom-call | flops 12884901888 | bytes 16777216 | tf_op jit(solution)/shard_map/conv/pallas_call | solution.py:296
  280.6 1.6 collective-permute-start.18
  282.4 1.5 collective-permute-start.20
  283.9 49.9 %conv.7 = (bf16[2,512,512]{2,1,0:T(8,128)(2,1)}, bf16[2,512,512]{2,1,0:T(8,128)(2,1)}, bf16[2,512,512]{2,1,0:T(8,128)(2,1)}, bf16[2,512,512]{2,1,0:T(8,128)(2,1)...) custom-call(s32[1]{0:T(128)} %bitcast.pos_ref, ...), custom_call_target="tpu_custom_call", output_to_operand_aliasing={{0}: (16, {}), {1}: (17, {}), {2}: (18, {}), {3}: (19, {}),... | custom-call | flops 12884901888 | bytes 16777216 | tf_op jit(solution)/shard_map/conv/pallas_call | solution.py:296
  333.9 1.5 collective-permute-start.21
  336.0 1.5 collective-permute-start.23
  337.5 18.9 %smooth.1 = (bf16[16384,256]{1,0:T(8,128)(2,1)}, f32[256,256]{1,0:T(8,128)}) custom-call(s32[1]{0:T(128)} %bitcast.pos_ref, bf16[16384,256]{1,0:T(8,128)(2,1)} %bitcast.73, bf16[16384,256]{1,0:T(8,128)(2,1)} %bitcast.77, bf16[256,768]{1,0:T(8,128)(2,1)} %w_ref.11, bf16[256,256]{1,0:T(8,128)(2,1)} %constant.87.clone.pick_ref, ...), custom_call_target="tpu_custom_call" | custom-call | flops 8589934592 | bytes 33554432 | tf_op jit(solution)/shard_map/smooth/pallas_call | solution.py:568
  356.4 3.8 collective-permute-done.21
  360.2 22.8 %collective-permute-done.22 = bf16[2,512,512]{2,1,0:T(8,128)(2,1)S(1)} collective-permute-done((bf16[2,512,512]{2,1,0:T(8,128)(2,1)}, bf16[2,512,512]{2,1,0:T(8,128)(2,1)S(1)}, u32[]{:S(2)}, u32[]{:S(2)}) %collective-permute-start.22) | collective-permute-done | bytes 1048608 | tf_op jit(solution)/shard_map/ppermute | solution.py:426
  383.1 1.4 collective-permute-start.31
  384.8 1.5 collective-permute-start.33
  386.4 11.8 %back.2.rest_5_ = f32[256,512]{1,0:T(8,128)} custom-call(s32[1]{0:T(128)} %bitcast.pos_ref, bf16[16384,256]{1,0:T(8,128)(2,1)} %bitcast.74, bf16[256,768]{1,0:T(8,128)(2,1)} %w_ref.11, bf16[256,256]{1,0:T(8,128)(2,1)} %constant.87.clone.pick_ref, bf16[2,32,16,512]{3,2,1,0:T(8,128)(2,1)} %bitcast.96, bf16[2,32,16,512]{3,2,1,0:T(8,128)(2,1)} %bitcast.99, ...), custom_call_target="tpu_custom_call" | custom-call | flops 4294967296 | bytes 16777216 | tf_op jit(solution)/shard_map/back/pallas_call | solution.py:588
  398.3 1.6 collective-permute-start.24
  399.9 4.5 collective-permute-done.24
  405.2 4.4 collective-permute-done.25
  409.5 2.4 collective-permute-start.26
  411.9 1.9 collective-permute-done.26
  413.9 1.2 collective-permute-done.27
  415.8 15.0 %collective-permute-done.28 = f32[64,256]{1,0:T(8,128)S(1)} collective-permute-done((f32[64,256]{1,0:T(8,128)S(1)}, f32[64,256]{1,0:T(8,128)S(1)}, u32[]{:S(2)}, u32[]{:S(2)}) %collective-permute-start.28) | collective-permute-done | bytes 65568 | tf_op jit(solution)/shard_map/ppermute | solution.py:471
  430.8 1.9 collective-permute-start.29
  432.7 2.9 collective-permute-done.29
  435.6 12.6 %back.3 = f32[256,512]{1,0:T(8,128)} custom-call(s32[1]{0:T(128)} %bitcast.pos_ref, bf16[16384,256]{1,0:T(8,128)(2,1)} %bitcast.75, bf16[256,768]{1,0:T(8,128)(2,1)} %w_ref.11, bf16[256,256]{1,0:T(8,128)(2,1)} %constant.87.clone.pick_ref, bf16[2,32,16,512]{3,2,1,0:T(8,128)(2,1)} %bitcast.41.rest_0_, bf16[2,32,16,512]{3,2,1,0:T(8,128)(2,1)} %bitcast.42.rest_1_, ...), custom_call_target="tpu_custom_call" | custom-call | flops 4294967296 | bytes 16777216 | tf_op jit(solution)/shard_map/back/pallas_call | solution.py:588
  449.4 1.6 collective-permute-start.34
  451.0 2.6 collective-permute-start.35
  453.6 1.4 collective-permute-start.36
  454.9 2.7 collective-permute-done.34
  457.7 4.6 collective-permute-done.35
  463.3 1.3 collective-permute-done.37
  465.8 4.5 collective-permute-done.38
  471.0 4.4 collective-permute-done.39
  (92 shorter events, 13.9 us)
Async XLA Ops:
  7.2 115.7 %all-gather.3.cloned.1.call-start = ((), (), s32[]{:S(2)}) async-start(), calls=%async_computation.1 | async-start | bytes 2621440 | tf_op jit(solution)/shard_map/all_gather | solution.py:550
  16.6 56.0 %collective-permute-start = (bf16[2,32,16,512]{3,2,1,0:T(8,128)(2,1)}, bf16[2,32,16,512]{3,2,1,0:T(8,128)(2,1)S(1)}, u32[]{:S(2)}, u32[]{:S(2)}) collective-permute-start(bf16[2,32,16,512]{3,2,1,0:T(8,128)(2,1)} %get-tuple-element.147), channel_id=1, source_target_pairs={{0,2},{1,3},{2,0},{3,1},{4,6},{5,7},{6,4},{7,5},{8,10},{9,11},{10,... | collective-permute-start | bytes 3145736 | tf_op jit(solution)/shard_map/ppermute | solution.py:426
  19.6 53.0 %collective-permute-start.1 = (bf16[2,32,16,512]{3,2,1,0:T(8,128)(2,1)}, bf16[2,32,16,512]{3,2,1,0:T(8,128)(2,1)}, u32[]{:S(2)}, u32[]{:S(2)}) collective-permute-start(bf16[2,32,16,512]{3,2,1,0:T(8,128)(2,1)} %get-tuple-element.148), channel_id=1, source_target_pairs={{0,4},{1,5},{2,6},{3,7},{4,0},{5,1},{6,2},{7,3},{8,12},{9,13},{10,... | collective-permute-start | bytes 3145736 | tf_op jit(solution)/shard_map/ppermute | solution.py:426
  21.1 51.5 %collective-permute-start.2 = (bf16[2,32,16,512]{3,2,1,0:T(8,128)(2,1)}, bf16[2,32,16,512]{3,2,1,0:T(8,128)(2,1)}, u32[]{:S(2)}, u32[]{:S(2)}) collective-permute-start(bf16[2,32,16,512]{3,2,1,0:T(8,128)(2,1)} %get-tuple-element.149), channel_id=1, source_target_pairs={{0,6},{1,7},{2,4},{3,5},{4,2},{5,3},{6,0},{7,1},{8,14},{9,15},{10,... | collective-permute-start | bytes 3145736 | tf_op jit(solution)/shard_map/ppermute | solution.py:426
  72.7 18.1 %collective-permute-start.6 = (bf16[2,32,16,512]{3,2,1,0:T(8,128)(2,1)}, bf16[2,32,16,512]{3,2,1,0:T(8,128)(2,1)S(1)}, u32[]{:S(2)}, u32[]{:S(2)}) collective-permute-start(bf16[2,32,16,512]{3,2,1,0:T(8,128)(2,1)} %get-tuple-element.160), channel_id=1, source_target_pairs={{0,1},{1,0},{2,3},{3,2},{4,5},{5,4},{6,7},{7,6},{8,9},{9,8},{10,11... | collective-permute-start | bytes 3145736 | tf_op jit(solution)/shard_map/ppermute | solution.py:426
  72.7 47.9 %collective-permute-start.8 = (bf16[2,32,16,512]{3,2,1,0:T(8,128)(2,1)}, bf16[2,32,16,512]{3,2,1,0:T(8,128)(2,1)S(1)}, u32[]{:S(2)}, u32[]{:S(2)}) collective-permute-start(bf16[2,32,16,512]{3,2,1,0:T(8,128)(2,1)} %get-tuple-element.164), channel_id=1, source_target_pairs={{0,5},{1,4},{2,7},{3,6},{4,1},{5,0},{6,3},{7,2},{8,13},{9,12},{10,... | collective-permute-start | bytes 3145736 | tf_op jit(solution)/shard_map/ppermute | solution.py:426
  74.4 48.5 %collective-permute-start.9 = (bf16[2,32,16,512]{3,2,1,0:T(8,128)(2,1)}, bf16[2,32,16,512]{3,2,1,0:T(8,128)(2,1)}, u32[]{:S(2)}, u32[]{:S(2)}) collective-permute-start(bf16[2,32,16,512]{3,2,1,0:T(8,128)(2,1)} %get-tuple-element.166), channel_id=1, source_target_pairs={{0,7},{1,6},{2,5},{3,4},{4,3},{5,2},{6,1},{7,0},{8,15},{9,14},{10,... | collective-permute-start | bytes 3145736 | tf_op jit(solution)/shard_map/ppermute | solution.py:426
  74.9 47.9 %collective-permute-start.7 = (bf16[2,32,16,512]{3,2,1,0:T(8,128)(2,1)}, bf16[2,32,16,512]{3,2,1,0:T(8,128)(2,1)}, u32[]{:S(2)}, u32[]{:S(2)}) collective-permute-start(bf16[2,32,16,512]{3,2,1,0:T(8,128)(2,1)} %get-tuple-element.162), channel_id=1, source_target_pairs={{0,3},{1,2},{2,1},{3,0},{4,7},{5,6},{6,5},{7,4},{8,11},{9,10},{10,... | collective-permute-start | bytes 3145736 | tf_op jit(solution)/shard_map/ppermute | solution.py:426
  89.8 83.0 %collective-permute-start.3 = (bf16[2,512,512]{2,1,0:T(8,128)(2,1)}, bf16[2,512,512]{2,1,0:T(8,128)(2,1)S(1)}, u32[]{:S(2)}, u32[]{:S(2)}) collective-permute-start(bf16[2,512,512]{2,1,0:T(8,128)(2,1)} %bitcast.111), channel_id=1, source_target_pairs={{0,2},{1,3},{2,0},{3,1},{4,6},{5,7},{6,4},{7,5},{8,10},{9,11},{10,... | collective-permute-start | bytes 3145736 | tf_op jit(solution)/shard_map/ppermute | solution.py:426
  91.7 81.0 %collective-permute-start.4 = (bf16[2,512,512]{2,1,0:T(8,128)(2,1)}, bf16[2,512,512]{2,1,0:T(8,128)(2,1)S(1)}, u32[]{:S(2)}, u32[]{:S(2)}) collective-permute-start(bf16[2,512,512]{2,1,0:T(8,128)(2,1)} %bitcast.110), channel_id=1, source_target_pairs={{0,4},{1,5},{2,6},{3,7},{4,0},{5,1},{6,2},{7,3},{8,12},{9,13},{10,... | collective-permute-start | bytes 3145736 | tf_op jit(solution)/shard_map/ppermute | solution.py:426
  121.6 51.1 %collective-permute-start.5 = (bf16[2,512,512]{2,1,0:T(8,128)(2,1)}, bf16[2,512,512]{2,1,0:T(8,128)(2,1)S(1)}, u32[]{:S(2)}, u32[]{:S(2)}) collective-permute-start(bf16[2,512,512]{2,1,0:T(8,128)(2,1)} %bitcast.109), channel_id=1, source_target_pairs={{0,6},{1,7},{2,4},{3,5},{4,2},{5,3},{6,0},{7,1},{8,14},{9,15},{10,... | collective-permute-start | bytes 3145736 | tf_op jit(solution)/shard_map/ppermute | solution.py:426
  172.7 54.0 %copy-start.6 = (bf16[2,512,512]{2,1,0:T(8,128)(2,1)}, bf16[2,512,512]{2,1,0:T(8,128)(2,1)S(1)}, u32[]{:S(2)}) copy-start(bf16[2,512,512]{2,1,0:T(8,128)(2,1)S(1)} %collective-permute-done.3.args_2_) | copy-start | bytes 3145732
  172.8 53.9 %copy-start.7 = (bf16[2,512,512]{2,1,0:T(8,128)(2,1)}, bf16[2,512,512]{2,1,0:T(8,128)(2,1)S(1)}, u32[]{:S(2)}) copy-start(bf16[2,512,512]{2,1,0:T(8,128)(2,1)S(1)} %collective-permute-done.4.args_4_) | copy-start | bytes 3145732
  172.8 53.9 %copy-start.8 = (bf16[2,512,512]{2,1,0:T(8,128)(2,1)}, bf16[2,512,512]{2,1,0:T(8,128)(2,1)S(1)}, u32[]{:S(2)}) copy-start(bf16[2,512,512]{2,1,0:T(8,128)(2,1)S(1)} %collective-permute-done.5.args_6_) | copy-start | bytes 3145732
  172.8 55.5 %collective-permute-start.13 = (bf16[2,512,512]{2,1,0:T(8,128)(2,1)}, bf16[2,512,512]{2,1,0:T(8,128)(2,1)}, u32[]{:S(2)}, u32[]{:S(2)}) collective-permute-start(bf16[2,512,512]{2,1,0:T(8,128)(2,1)} %bitcast.106), channel_id=1, source_target_pairs={{0,1},{1,0},{2,3},{3,2},{4,5},{5,4},{6,7},{7,6},{8,9},{9,8},{10,11... | collective-permute-start | bytes 3145736 | tf_op jit(solution)/shard_map/ppermute | solution.py:426
  173.9 54.8 %collective-permute-start.14 = (bf16[2,512,512]{2,1,0:T(8,128)(2,1)}, bf16[2,512,512]{2,1,0:T(8,128)(2,1)}, u32[]{:S(2)}, u32[]{:S(2)}) collective-permute-start(bf16[2,512,512]{2,1,0:T(8,128)(2,1)} %bitcast.103), channel_id=1, source_target_pairs={{0,3},{1,2},{2,1},{3,0},{4,7},{5,6},{6,5},{7,4},{8,11},{9,10},{10,... | collective-permute-start | bytes 3145736 | tf_op jit(solution)/shard_map/ppermute | solution.py:426
  175.1 55.2 %collective-permute-start.15 = (bf16[2,512,512]{2,1,0:T(8,128)(2,1)}, bf16[2,512,512]{2,1,0:T(8,128)(2,1)}, u32[]{:S(2)}, u32[]{:S(2)}) collective-permute-start(bf16[2,512,512]{2,1,0:T(8,128)(2,1)} %bitcast.102), channel_id=1, source_target_pairs={{0,5},{1,4},{2,7},{3,6},{4,1},{5,0},{6,3},{7,2},{8,13},{9,12},{10,... | collective-permute-start | bytes 3145736 | tf_op jit(solution)/shard_map/ppermute | solution.py:426
  175.7 54.6 %collective-permute-start.16 = (bf16[2,512,512]{2,1,0:T(8,128)(2,1)}, bf16[2,512,512]{2,1,0:T(8,128)(2,1)}, u32[]{:S(2)}, u32[]{:S(2)}) collective-permute-start(bf16[2,512,512]{2,1,0:T(8,128)(2,1)} %bitcast.101), channel_id=1, source_target_pairs={{0,7},{1,6},{2,5},{3,4},{4,3},{5,2},{6,1},{7,0},{8,15},{9,14},{10,... | collective-permute-start | bytes 3145736 | tf_op jit(solution)/shard_map/ppermute | solution.py:426
  226.7 53.7 %collective-permute-start.10 = (bf16[2,512,512]{2,1,0:T(8,128)(2,1)}, bf16[2,512,512]{2,1,0:T(8,128)(2,1)S(1)}, u32[]{:S(2)}, u32[]{:S(2)}) collective-permute-start(bf16[2,512,512]{2,1,0:T(8,128)(2,1)} %get-tuple-element.195), channel_id=1, source_target_pairs={{0,2},{1,3},{2,0},{3,1},{4,6},{5,7},{6,4},{7,5},{8,10},{9,11},{10,... | collective-permute-start | bytes 3145736 | tf_op jit(solution)/shard_map/ppermute | solution.py:426
  228.3 52.2 %collective-permute-start.11 = (bf16[2,512,512]{2,1,0:T(8,128)(2,1)}, bf16[2,512,512]{2,1,0:T(8,128)(2,1)S(1)}, u32[]{:S(2)}, u32[]{:S(2)}) collective-permute-start(bf16[2,512,512]{2,1,0:T(8,128)(2,1)} %get-tuple-element.197), channel_id=1, source_target_pairs={{0,4},{1,5},{2,6},{3,7},{4,0},{5,1},{6,2},{7,3},{8,12},{9,13},{10,... | collective-permute-start | bytes 3145736 | tf_op jit(solution)/shard_map/ppermute | solution.py:426
  228.8 51.7 %collective-permute-start.12 = (bf16[2,512,512]{2,1,0:T(8,128)(2,1)}, bf16[2,512,512]{2,1,0:T(8,128)(2,1)S(1)}, u32[]{:S(2)}, u32[]{:S(2)}) collective-permute-start(bf16[2,512,512]{2,1,0:T(8,128)(2,1)} %get-tuple-element.199), channel_id=1, source_target_pairs={{0,6},{1,7},{2,4},{3,5},{4,2},{5,3},{6,0},{7,1},{8,14},{9,15},{10,... | collective-permute-start | bytes 3145736 | tf_op jit(solution)/shard_map/ppermute | solution.py:426
  280.5 53.4 %copy-start.3 = (bf16[2,512,512]{2,1,0:T(8,128)(2,1)}, bf16[2,512,512]{2,1,0:T(8,128)(2,1)S(1)}, u32[]{:S(2)}) copy-start(bf16[2,512,512]{2,1,0:T(8,128)(2,1)S(1)} %collective-permute-done.10) | copy-start | bytes 3145732
  280.5 53.4 %copy-start.4 = (bf16[2,512,512]{2,1,0:T(8,128)(2,1)}, bf16[2,512,512]{2,1,0:T(8,128)(2,1)S(1)}, u32[]{:S(2)}) copy-start(bf16[2,512,512]{2,1,0:T(8,128)(2,1)S(1)} %collective-permute-done.11) | copy-start | bytes 3145732
  280.5 53.4 %copy-start.5 = (bf16[2,512,512]{2,1,0:T(8,128)(2,1)}, bf16[2,512,512]{2,1,0:T(8,128)(2,1)S(1)}, u32[]{:S(2)}) copy-start(bf16[2,512,512]{2,1,0:T(8,128)(2,1)S(1)} %collective-permute-done.12) | copy-start | bytes 3145732
  280.5 54.9 %collective-permute-start.17 = (bf16[2,512,512]{2,1,0:T(8,128)(2,1)}, bf16[2,512,512]{2,1,0:T(8,128)(2,1)}, u32[]{:S(2)}, u32[]{:S(2)}) collective-permute-start(bf16[2,512,512]{2,1,0:T(8,128)(2,1)} %get-tuple-element.237), channel_id=1, source_target_pairs={{0,1},{1,0},{2,3},{3,2},{4,5},{5,4},{6,7},{7,6},{8,9},{9,8},{10,11... | collective-permute-start | bytes 3145736 | tf_op jit(solution)/shard_map/ppermute | solution.py:426
  280.6 55.3 %collective-permute-start.18 = (bf16[2,512,512]{2,1,0:T(8,128)(2,1)}, bf16[2,512,512]{2,1,0:T(8,128)(2,1)}, u32[]{:S(2)}, u32[]{:S(2)}) collective-permute-start(bf16[2,512,512]{2,1,0:T(8,128)(2,1)} %get-tuple-element.239), channel_id=1, source_target_pairs={{0,3},{1,2},{2,1},{3,0},{4,7},{5,6},{6,5},{7,4},{8,11},{9,10},{10,... | collective-permute-start | bytes 3145736 | tf_op jit(solution)/shard_map/ppermute | solution.py:426
  282.2 55.2 %collective-permute-start.19 = (bf16[2,512,512]{2,1,0:T(8,128)(2,1)}, bf16[2,512,512]{2,1,0:T(8,128)(2,1)}, u32[]{:S(2)}, u32[]{:S(2)}) collective-permute-start(bf16[2,512,512]{2,1,0:T(8,128)(2,1)} %get-tuple-element.241), channel_id=1, source_target_pairs={{0,5},{1,4},{2,7},{3,6},{4,1},{5,0},{6,3},{7,2},{8,13},{9,12},{10,... | collective-permute-start | bytes 3145736 | tf_op jit(solution)/shard_map/ppermute | solution.py:426
  282.4 55.1 %collective-permute-start.20 = (bf16[2,512,512]{2,1,0:T(8,128)(2,1)}, bf16[2,512,512]{2,1,0:T(8,128)(2,1)}, u32[]{:S(2)}, u32[]{:S(2)}) collective-permute-start(bf16[2,512,512]{2,1,0:T(8,128)(2,1)} %get-tuple-element.243), channel_id=1, source_target_pairs={{0,7},{1,6},{2,5},{3,4},{4,3},{5,2},{6,1},{7,0},{8,15},{9,14},{10,... | collective-permute-start | bytes 3145736 | tf_op jit(solution)/shard_map/ppermute | solution.py:426
  333.9 26.3 %collective-permute-start.21 = (bf16[2,512,512]{2,1,0:T(8,128)(2,1)}, bf16[2,512,512]{2,1,0:T(8,128)(2,1)S(1)}, u32[]{:S(2)}, u32[]{:S(2)}) collective-permute-start(bf16[2,512,512]{2,1,0:T(8,128)(2,1)} %get-tuple-element.247), channel_id=1, source_target_pairs={{0,2},{1,3},{2,0},{3,1},{4,6},{5,7},{6,4},{7,5},{8,10},{9,11},{10,... | collective-permute-start | bytes 3145736 | tf_op jit(solution)/shard_map/ppermute | solution.py:426
  335.4 47.5 %collective-permute-start.22 = (bf16[2,512,512]{2,1,0:T(8,128)(2,1)}, bf16[2,512,512]{2,1,0:T(8,128)(2,1)S(1)}, u32[]{:S(2)}, u32[]{:S(2)}) collective-permute-start(bf16[2,512,512]{2,1,0:T(8,128)(2,1)} %get-tuple-element.249), channel_id=1, source_target_pairs={{0,4},{1,5},{2,6},{3,7},{4,0},{5,1},{6,2},{7,3},{8,12},{9,13},{10,... | collective-permute-start | bytes 3145736 | tf_op jit(solution)/shard_map/ppermute | solution.py:426
  336.0 47.0 %collective-permute-start.23 = (bf16[2,512,512]{2,1,0:T(8,128)(2,1)}, bf16[2,512,512]{2,1,0:T(8,128)(2,1)S(1)}, u32[]{:S(2)}, u32[]{:S(2)}) collective-permute-start(bf16[2,512,512]{2,1,0:T(8,128)(2,1)} %get-tuple-element.251), channel_id=1, source_target_pairs={{0,6},{1,7},{2,4},{3,5},{4,2},{5,3},{6,0},{7,1},{8,14},{9,15},{10,... | collective-permute-start | bytes 3145736 | tf_op jit(solution)/shard_map/ppermute | solution.py:426
  383.0 52.6 %collective-permute-start.30 = (bf16[2,512,512]{2,1,0:T(8,128)(2,1)}, bf16[2,512,512]{2,1,0:T(8,128)(2,1)}, u32[]{:S(2)}, u32[]{:S(2)}) collective-permute-start(bf16[2,512,512]{2,1,0:T(8,128)(2,1)} %get-tuple-element.262), channel_id=1, source_target_pairs={{0,3},{1,2},{2,1},{3,0},{4,7},{5,6},{6,5},{7,4},{8,11},{9,10},{10,... | collective-permute-start | bytes 3145736 | tf_op jit(solution)/shard_map/ppermute | solution.py:426
  383.1 52.5 %collective-permute-start.31 = (bf16[2,512,512]{2,1,0:T(8,128)(2,1)}, bf16[2,512,512]{2,1,0:T(8,128)(2,1)}, u32[]{:S(2)}, u32[]{:S(2)}) collective-permute-start(bf16[2,512,512]{2,1,0:T(8,128)(2,1)} %get-tuple-element.263), channel_id=1, source_target_pairs={{0,5},{1,4},{2,7},{3,6},{4,1},{5,0},{6,3},{7,2},{8,13},{9,12},{10,... | collective-permute-start | bytes 3145736 | tf_op jit(solution)/shard_map/ppermute | solution.py:426
  384.4 51.2 %collective-permute-start.32 = (bf16[2,512,512]{2,1,0:T(8,128)(2,1)}, bf16[2,512,512]{2,1,0:T(8,128)(2,1)}, u32[]{:S(2)}, u32[]{:S(2)}) collective-permute-start(bf16[2,512,512]{2,1,0:T(8,128)(2,1)} %get-tuple-element.264), channel_id=1, source_target_pairs={{0,7},{1,6},{2,5},{3,4},{4,3},{5,2},{6,1},{7,0},{8,15},{9,14},{10,... | collective-permute-start | bytes 3145736 | tf_op jit(solution)/shard_map/ppermute | solution.py:426
  384.8 50.8 %collective-permute-start.33 = (bf16[2,512,512]{2,1,0:T(8,128)(2,1)}, bf16[2,512,512]{2,1,0:T(8,128)(2,1)}, u32[]{:S(2)}, u32[]{:S(2)}) collective-permute-start(bf16[2,512,512]{2,1,0:T(8,128)(2,1)} %get-tuple-element.265), channel_id=1, source_target_pairs={{0,1},{1,0},{2,3},{3,2},{4,5},{5,4},{6,7},{7,6},{8,9},{9,8},{10,11... | collective-permute-start | bytes 3145736 | tf_op jit(solution)/shard_map/ppermute | solution.py:426
  398.3 6.1 %collective-permute-start.24 = (f32[64,256]{1,0:T(8,128)S(1)}, f32[64,256]{1,0:T(8,128)S(1)}, u32[]{:S(2)}, u32[]{:S(2)}) collective-permute-start(f32[64,256]{1,0:T(8,128)S(1)} %get-tuple-element.271), channel_id=1, source_target_pairs={{0,8},{8,16},{16,24},{24,0},{1,9},{9,17},{17,25},{25,1},{2,10},{10... | collective-permute-start | bytes 196616 | tf_op jit(solution)/shard_map/ppermute | solution.py:462
  404.4 5.2 %collective-permute-start.25 = (f32[64,256]{1,0:T(8,128)S(1)}, f32[64,256]{1,0:T(8,128)S(1)}, u32[]{:S(2)}, u32[]{:S(2)}) collective-permute-start(f32[64,256]{1,0:T(8,128)S(1)} %get-tuple-element.273), channel_id=1, source_target_pairs={{0,16},{8,24},{16,0},{24,8},{1,17},{9,25},{17,1},{25,9},{2,18},{10... | collective-permute-start | bytes 196616 | tf_op jit(solution)/shard_map/ppermute | solution.py:462
  409.5 4.3 collective-permute-start.26
  413.9 1.3 collective-permute-start.27
  415.2 15.6 %collective-permute-start.28 = (f32[64,256]{1,0:T(8,128)S(1)}, f32[64,256]{1,0:T(8,128)S(1)}, u32[]{:S(2)}, u32[]{:S(2)}) collective-permute-start(f32[64,256]{1,0:T(8,128)S(1)} %add.96), channel_id=1, source_target_pairs={{0,2},{1,3},{2,0},{3,1},{4,6},{5,7},{6,4},{7,5},{8,10},{9,11},{10,... | collective-permute-start | bytes 196616 | tf_op jit(solution)/shard_map/ppermute | solution.py:471
  430.8 4.8 collective-permute-start.29
  448.3 27.2 %copy-start = (bf16[256,256]{1,0:T(8,128)(2,1)S(1)}, bf16[256,256]{1,0:T(8,128)(2,1)}, u32[]{:S(2)}) copy-start(bf16[256,256]{1,0:T(8,128)(2,1)} %constant.87.clone.pick_ref) | copy-start | bytes 393220
  449.4 8.3 %collective-permute-start.34 = (f32[64,512]{1,0:T(8,128)S(1)}, f32[64,512]{1,0:T(8,128)S(1)}, u32[]{:S(2)}, u32[]{:S(2)}) collective-permute-start(f32[64,512]{1,0:T(8,128)S(1)} %get-tuple-element.268), channel_id=1, source_target_pairs={{0,8},{8,16},{16,24},{24,0},{1,9},{9,17},{17,25},{25,1},{2,10},{10... | collective-permute-start | bytes 393224 | tf_op jit(solution)/shard_map/ppermute | solution.py:462
  451.0 11.3 %collective-permute-start.35 = (f32[64,512]{1,0:T(8,128)S(1)}, f32[64,512]{1,0:T(8,128)S(1)}, u32[]{:S(2)}, u32[]{:S(2)}) collective-permute-start(f32[64,512]{1,0:T(8,128)S(1)} %get-tuple-element.270), channel_id=1, source_target_pairs={{0,16},{8,24},{16,0},{24,8},{1,17},{9,25},{17,1},{25,9},{2,18},{10... | collective-permute-start | bytes 393224 | tf_op jit(solution)/shard_map/ppermute | solution.py:462
  453.6 8.7 %collective-permute-start.36 = (f32[64,512]{1,0:T(8,128)S(1)}, f32[64,512]{1,0:T(8,128)S(1)}, u32[]{:S(2)}, u32[]{:S(2)}) collective-permute-start(f32[64,512]{1,0:T(8,128)S(1)} %get-tuple-element.269), channel_id=1, source_target_pairs={{0,24},{8,0},{16,8},{24,16},{1,25},{9,1},{17,9},{25,17},{2,26},{10... | collective-permute-start | bytes 393224 | tf_op jit(solution)/shard_map/ppermute | solution.py:462
  463.2 1.4 collective-permute-start.37
  464.7 5.6 %collective-permute-start.38 = (f32[64,512]{1,0:T(8,128)S(1)}, f32[64,512]{1,0:T(8,128)S(1)}, u32[]{:S(2)}, u32[]{:S(2)}) collective-permute-start(f32[64,512]{1,0:T(8,128)S(1)} %add.102), channel_id=1, source_target_pairs={{0,2},{1,3},{2,0},{3,1},{4,6},{5,7},{6,4},{7,5},{8,10},{9,11},{10,... | collective-permute-start | bytes 393224 | tf_op jit(solution)/shard_map/ppermute | solution.py:471
  470.3 5.0 %collective-permute-start.39 = (f32[64,512]{1,0:T(8,128)S(1)}, f32[64,512]{1,0:T(8,128)S(1)}, u32[]{:S(2)}, u32[]{:S(2)}) collective-permute-start(f32[64,512]{1,0:T(8,128)S(1)} %add.103), channel_id=1, source_target_pairs={{0,4},{1,5},{2,6},{3,7},{4,0},{5,1},{6,2},{7,3},{8,12},{9,13},{10,... | collective-permute-start | bytes 393224 | tf_op jit(solution)/shard_map/ppermute | solution.py:471
  (8 other events, 77.8 us)
Sparse Core Ops, SparseCore 0:
  72.8 46.0 all-gather.2

commit v2 on v1

--- a/solution.py
+++ b/solution.py
@@ -146,33 +146,28 @@
 
 def convolve(signal, refs, filt_real, filt_imag, orient, hold_ref):
     first_ref, second_ref, third_ref, fourth_ref, cos_ref, sin_ref = refs
-    n_one = cos_ref.shape[0]
-    n_two = cos_ref.shape[1]
-    block = n_one // 2
-    for start in range(0, n_one, block):
-        span = slice(start, start + block)
-        low = slice(n_one + start, n_one + start + block)
-        cos, sin = cos_ref[span, :], sin_ref[span, :]
-        real = dot_nn(first_ref[span, :], signal)
-        imag = dot_nn(first_ref[low, :], signal)
-        turned = jnp.concatenate(
-            [(real * cos + imag * sin).astype(BF), (imag * cos - real * sin).astype(BF)], axis=1
-        )
-        spec = dot_nn(turned, second_ref[...])
-        real, imag = spec[:, :n_two], spec[:, n_two:]
-        f_real = filt_real(span).astype(F32)
-        f_imag = filt_imag(span).astype(F32) * orient
-        product = jnp.concatenate(
-            [
-                (real * f_real - imag * f_imag).astype(BF),
-                (real * f_imag + imag * f_real).astype(BF),
-            ],
-            axis=1,
-        )
-        back = dot_nn(product, third_ref[...])
-        real, imag = back[:, :n_two], back[:, n_two:]
-        hold_ref[span, :] = (real * cos - imag * sin).astype(BF)
-        hold_ref[low, :] = (imag * cos + real * sin).astype(BF)
+    n_one, n_two = cos_ref.shape
+    cos, sin = cos_ref[...], sin_ref[...]
+    partial = dot_nn(first_ref[...], signal)
+    real, imag = partial[:n_one], partial[n_one:]
+    turned = jnp.concatenate(
+        [(real * cos + imag * sin).astype(BF), (imag * cos - real * sin).astype(BF)], axis=1
+    )
+    spec = dot_nn(turned, second_ref[...])
+    real, imag = spec[:, :n_two], spec[:, n_two:]
+    f_real = filt_real.astype(F32)
+    f_imag = filt_imag.astype(F32) * orient
+    product = jnp.concatenate(
+        [
+            (real * f_real - imag * f_imag).astype(BF),
+            (real * f_imag + imag * f_real).astype(BF),
+        ],
+        axis=1,
+    )
+    back = dot_nn(product, third_ref[...])
+    real, imag = back[:, :n_two], back[:, n_two:]
+    hold_ref[:n_one, :] = (real * cos - imag * sin).astype(BF)
+    hold_ref[n_one:, :] = (imag * cos + real * sin).astype(BF)
     return dot_nn(fourth_ref[...], hold_ref[...])
 
 
@@ -219,8 +214,8 @@
     result = convolve(
         signal,
         tables,
-        lambda span: filt_ref[0, span, :],
-        lambda span: filt_ref[1, span, :],
+        filt_ref[0],
+        filt_ref[1],
         orient,
         hold_ref,
     )
@@ -250,8 +245,8 @@
     out_ref[0] = convolve(
         x_ref[0],
         (first, second, third, fourth, cos, sin),
-        lambda span: fr_ref[0, span, :],
-        lambda span: fi_ref[0, span, :],
+        fr_ref[0],
+        fi_ref[0],
         orient,
         hold_ref,
     ).astype(BF)
@@ -338,7 +333,7 @@
     return result.reshape(blocks.shape)
 
 
-def store_sum(pos_ref, total, sum_ref, turn_ref, peers, blocks, chunks, rows):
+def store_sum(pos_ref, total, outs, turn_ref, flat_ref, peers, blocks, chunks, rows, earlier):
     pos = pos_ref[0]
     kinds = total.shape[0] // (len(blocks) * chunks * rows)
     spot = 0
@@ -351,11 +346,25 @@
                 span = pl.ds(pl.multiple_of(start, rows), rows)
                 turn_ref[span, :] = total[spot : spot + rows]
                 spot += rows
-    sum_ref[...] = turn_ref[...].T
+    summed = turn_ref[...].T
+    for ref in earlier:
+        summed = summed + ref[...]
+    if len(outs) == 1:
+        outs[0][...] = summed
+        return
+    flat_ref[...] = summed
+    keep_ref, sent_ref = outs
+    groups, size, _ = keep_ref.shape
+    core = pos % 2
+    for group in range(groups):
+        base = lax.rem(pos_ref[1] + group, groups) * (2 * size)
+        keep_ref[group] = flat_ref[pl.ds(pl.multiple_of(base + core * size, size), size), :]
+        sent_ref[group] = flat_ref[pl.ds(pl.multiple_of(base + (1 - core) * size, size), size), :]
 
 
 def smooth_kernel(pos_ref, tok_ref, cot_ref, w_ref, pick_ref, *rest):
-    parts, (gated_ref, sum_ref, held_ref, wt_ref, total_ref, turn_ref) = rest[:-6], rest[-6:]
+    parts, (gated_ref, *outs) = rest[:-7], rest[-7:-4]
+    held_ref, wt_ref, total_ref, turn_ref = rest[-4:]
     chunks, steps, rows, width = parts[0].shape
     peers = len(parts)
     chan = pick_ref.shape[1]
@@ -379,37 +388,69 @@
 
     @pl.when(pl.program_id(0) == pl.num_programs(0) - 1)
     def _():
-        store_sum(pos_ref, total, sum_ref, turn_ref, peers, range(peers), chunks, rows)
-
-
-def back_kernel(pos_ref, tok_ref, w_ref, pick_ref, *rest, peers, blocks):
-    parts, rest = rest[: len(blocks)], rest[len(blocks) :]
-    earlier, (sum_ref, held_ref, wt_ref, total_ref, turn_ref) = rest[:-5], rest[-5:]
+        store_sum(
+            pos_ref, total, outs, turn_ref, total_ref, peers, range(peers), chunks, rows, []
+        )
+
+
+def back_terms(parts, feats, tokens, step):
+    count = feats.shape[0] // 2
+    mixed = load_blocks(parts, step)
+    grads = [mixed * feats[count:], mixed * feats[:count]]
+    return dot_nn(jnp.concatenate([grad.astype(BF) for grad in grads], axis=0), tokens)
+
+
+def back_first_kernel(pos_ref, tok_ref, w_ref, pick_ref, *rest, peers, blocks, others):
+    parts, (sum_ref, feat_ref) = rest[: len(blocks)], rest[len(blocks) : -5]
+    held_ref, later_ref, wt_ref, total_ref, turn_ref = rest[-5:]
     chunks, steps, rows, width = parts[0].shape
-    count = len(blocks) * chunks * rows
+    count = 2 * held_ref.shape[0]
 
     @pl.when(pl.program_id(0) == 0)
     def _():
         gather_rows(pos_ref, pick_ref, held_ref, peers, blocks, rows)
-        key_value_weights(w_ref, held_ref, wt_ref)
+        gather_rows(pos_ref, pick_ref, later_ref, peers, others, rows)
+        key_value_weights(w_ref, held_ref, wt_ref.at[:count])
+        key_value_weights(w_ref, later_ref, wt_ref.at[count:])
         total_ref[...] = jnp.zeros_like(total_ref)
 
     total = total_ref[...]
     for step in range(steps):
-        tokens = tok_ref[step * width : (step + 1) * width, :]
-        feats = rounded(dot_nt(wt_ref[...], tokens))
-        mixed = load_blocks(parts, step)
-        grads = jnp.concatenate(
-            [(mixed * feats[count:]).astype(BF), (mixed * feats[:count]).astype(BF)], axis=0
-        )
-        total = total + dot_nn(grads, tokens)
+        span = slice(step * width, (step + 1) * width)
+        tokens = tok_ref[span, :]
+        feats = dot_nt(wt_ref[...], tokens).astype(BF)
+        feat_ref[:, span] = feats[count:]
+        total = total + back_terms(parts, feats[:count].astype(F32), tokens, step)
     total_ref[...] = total
 
     @pl.when(pl.program_id(0) == pl.num_programs(0) - 1)
     def _():
-        store_sum(pos_ref, total, sum_ref, turn_ref, peers, blocks, chunks, rows)
-        for ref in earlier:
-            sum_ref[...] += ref[...]
+        store_sum(
+            pos_ref, total, [sum_ref], turn_ref, None, peers, blocks, chunks, rows, []
+        )
+
+
+def back_last_kernel(pos_ref, tok_ref, feat_ref, earlier_ref, *rest, peers, blocks):
+    parts, outs = rest[: len(blocks)], rest[len(blocks) : -3]
+    total_ref, turn_ref, flat_ref = rest[-3:]
+    chunks, steps, rows, width = parts[0].shape
+
+    @pl.when(pl.program_id(0) == 0)
+    def _():
+        total_ref[...] = jnp.zeros_like(total_ref)
+
+    total = total_ref[...]
+    for step in range(steps):
+        span = slice(step * width, (step + 1) * width)
+        feats = feat_ref[:, span].astype(F32)
+        total = total + back_terms(parts, feats, tok_ref[span, :], step)
+    total_ref[...] = total
+
+    @pl.when(pl.program_id(0) == pl.num_programs(0) - 1)
+    def _():
+        store_sum(
+            pos_ref, total, outs, turn_ref, flat_ref, peers, blocks, chunks, rows, [earlier_ref]
+        )
 
 
 def halves(peers):
@@ -473,6 +514,31 @@
     return value
 
 
+def swap(value, step):
+    pairs = [(device, device ^ step) for device in range(lax.axis_size("ctx"))]
+    return lax.ppermute(value, "ctx", pairs)
+
+
+def reduce_kept(keep, sent):
+    keep = keep + swap(sent, 1)
+    groups = lax.axis_size("dp")
+    total = keep[0]
+    for step in range(1, groups):
+        pairs = [(device, (device + step) % groups) for device in range(groups)]
+        total = total + lax.ppermute(keep[step], "dp", pairs)
+    return total
+
+
+def reduce_chips(total):
+    step = 2
+    while step < lax.axis_size("ctx"):
+        total = total + swap(total, step)
+        step *= 2
+    other = swap(total, 1)
+    upper = lax.axis_index("ctx") % 2 != 0
+    return jnp.concatenate([jnp.where(upper, other, total), jnp.where(upper, total, other)])
+
+
 def with_kernels(arrays, tables, pick, chunks, repeats, group_pos):
     tokens, cotangent, w_in, filter_real, filter_imag = arrays
     peers = lax.axis_size("ctx")
@@ -482,12 +548,17 @@
     rows = chan // (peers * chunks)
     count = peers * rows
     me = lax.axis_index("ctx").astype(jnp.int32)
-    pos = me.reshape(1)
-    steps = math.gcd(shard_rows, 4)
-    grid = (shard_rows // steps,)
-    tok_spec = pl.BlockSpec((steps * width, chan), lambda i: (i, 0))
-    part_spec = pl.BlockSpec((chunks, steps, rows, width), lambda i: (0, i, 0, 0))
-    chunk_spec = pl.BlockSpec((1, steps, rows, width), lambda i: (0, i, 0, 0))
+    pos = jnp.stack([me, group_pos.astype(jnp.int32)])
+    groups = lax.axis_size("dp")
+
+    def specs(most):
+        steps = math.gcd(shard_rows, most)
+        return (
+            (shard_rows // steps,),
+            pl.BlockSpec((steps * width, chan), lambda i: (i, 0)),
+            pl.BlockSpec((chunks, steps, rows, width), lambda i: (0, i, 0, 0)),
+        )
+
     part_out = jax.ShapeDtypeStruct((chunks, shard_rows, rows, width), BF)
     w_spec, pick_spec = whole(w_in.shape), whole(pick.shape)
     macs = tok_rows * chan * chan
@@ -513,6 +584,7 @@
 
     mixed = [None] * peers
     last = pos
+    grid, tok_spec, part_spec = specs(16)
     for group in (first_group, second_group):
         some = len(group) * chunks * rows
         outs = pl.pallas_call(
@@ -536,6 +608,7 @@
     (last, mine), held_back = after([arrived[block] for block in early], (last, mine))
     for block, value in zip(early, held_back):
         arrived[block] = value
+    grid, tok_spec, part_spec = specs(8)
     grads = list(pl.pallas_call(
         functools.partial(grad_kernel, peers=peers),
         grid=grid,
@@ -565,45 +638,67 @@
     last, back = after(back, pos)
     back = send(back, early)
 
-    gated, gate_sum = pl.pallas_call(
+    def kept(cols):
+        shape = (groups, chan // groups // 2, cols)
+        return (
+            [pl.BlockSpec(shape, lambda i: (0, 0, 0))] * 2, [jax.ShapeDtypeStruct(shape, F32)] * 2
+        )
+
+    kept_specs, kept_shapes = kept(chan)
+    gated, *gate_sum = pl.pallas_call(
         smooth_kernel,
         grid=grid,
         in_specs=[POS_SPEC, tok_spec, tok_spec, w_spec, pick_spec] + [part_spec] * peers,
-        out_specs=[tok_spec, pl.BlockSpec((chan, chan), lambda i: (0, 0))],
-        out_shape=[
-            jax.ShapeDtypeStruct((tok_rows, chan), BF), jax.ShapeDtypeStruct((chan, chan), F32)
-        ],
+        out_specs=[tok_spec] + kept_specs,
+        out_shape=[jax.ShapeDtypeStruct((tok_rows, chan), BF)] + kept_shapes,
         scratch_shapes=[held(chan), held(chan), held(chan, F32), held(chan, F32)],
         compiler_params=params(),
         cost_estimate=cost(4, 4),
         name="smooth",
     )(last, tokens, cotangent, w_in, pick, *shaped(smooth, part_out.shape))
-    (last, back), gate_sum = after(gate_sum, (pos, back))
+    back, gate_sum = after(gate_sum, back)
+    gate_sum = reduce_kept(*gate_sum)
+    last, gate_sum = after(gate_sum, pos)
     back = send(back, late)
+
     sum_shape = (chan, 2 * chan)
-    back_sum = []
-    for group in (early, late):
-        some = len(group) * chunks * rows
-        blocks = shaped([back[block] for block in group], part_out.shape)
-        back_sum = [pl.pallas_call(
-            functools.partial(back_kernel, peers=peers, blocks=group),
-            grid=grid,
-            in_specs=[POS_SPEC, tok_spec, w_spec, pick_spec] + [part_spec] * len(group)
-            + [whole(sum_shape)] * len(back_sum),
-            out_specs=pl.BlockSpec(sum_shape, lambda i: (0, 0)),
-            out_shape=jax.ShapeDtypeStruct(sum_shape, F32),
-            scratch_shapes=[
-                held(some), held(2 * some), held(2 * some, F32), held(2 * chan, F32)
-            ],
-            compiler_params=params(),
-            cost_estimate=cost(2, 2),
-            name="back",
-        )(last, tokens, w_in, pick, *blocks, *back_sum)]
-        if group == early:
-            gate_sum, back_sum = after(back_sum, gate_sum)
-            gate_sum = reduce_tokens(reduce_groups(gate_sum))
-            last, gate_sum = after(gate_sum, pos)
-    return gated, gate_sum, reduce_tokens(reduce_groups(back_sum[0]))
+    grid, tok_spec, part_spec = specs(8)
+    some, others = len(early) * chunks * rows, len(late) * chunks * rows
+    steps = tok_spec.block_shape[0]
+    feat_spec = pl.BlockSpec((2 * others, steps), lambda i: (0, i))
+    back_sum, feats = pl.pallas_call(
+        functools.partial(back_first_kernel, peers=peers, blocks=early, others=late),
+        grid=grid,
+        in_specs=[POS_SPEC, tok_spec, w_spec, pick_spec] + [part_spec] * len(early),
+        out_specs=[pl.BlockSpec(sum_shape, lambda i: (0, 0)), feat_spec],
+        out_shape=[
+            jax.ShapeDtypeStruct(sum_shape, F32),
+            jax.ShapeDtypeStruct((2 * others, tok_rows), BF),
+        ],
+        scratch_shapes=[
+            held(some), held(others), held(2 * (some + others)), held(2 * some, F32),
+            held(2 * chan, F32),
+        ],
+        compiler_params=params(),
+        cost_estimate=cost(3, 3),
+        name="back_first",
+    )(last, tokens, w_in, pick, *shaped([back[block] for block in early], part_out.shape))
+    kept_specs, kept_shapes = kept(2 * chan)
+    back_sum = pl.pallas_call(
+        functools.partial(back_last_kernel, peers=peers, blocks=late),
+        grid=grid,
+        in_specs=[POS_SPEC, tok_spec, feat_spec, whole(sum_shape)] + [part_spec] * len(late),
+        out_specs=kept_specs,
+        out_shape=kept_shapes,
+        scratch_shapes=[
+            held(2 * others, F32), held(2 * chan, F32), pltpu.VMEM(sum_shape, F32)
+        ],
+        compiler_params=params(),
+        cost_estimate=cost(1, 2.5),
+        name="back_last",
+    )(pos, tokens, feats, back_sum, *shaped([back[block] for block in late], part_out.shape))
+    summed = jnp.concatenate([gate_sum, reduce_kept(*back_sum)], axis=1)
+    return gated, reduce_chips(summed)
 
 
 def without_kernels(arrays, tables, pick, rows, repeats, group_pos):
@@ -634,7 +729,7 @@
     terms = [cot * smooth, back * value, back * key]
     sums = [dot_nn(term.astype(BF), tokens).T for term in terms]
     summed = reduce_tokens(reduce_groups(jnp.concatenate(sums, axis=1)))
-    return gated, summed[:, :chan], summed[:, chan:]
+    return gated, summed
 
 
 def per_device(inputs, grad_out, w_in, filter_real, filter_imag):
@@ -667,17 +762,16 @@
     group_pos = lax.axis_index("dp")
     arrays = (tokens, cotangent, w_in, filter_real, filter_imag)
     if use_kernels:
-        gated, gate_sum, back_sum = with_kernels(
+        gated, summed = with_kernels(
             arrays, tables, pick, chunks, repeats, group_pos
         )
     else:
-        gated, gate_sum, back_sum = without_kernels(
+        gated, summed = without_kernels(
             arrays, tables, pick, rows, repeats, group_pos
         )
 
     scale = 1.0 / math.sqrt(inputs.shape[0] * group_count * seq_len)
 
-    summed = jnp.concatenate([gate_sum, back_sum], axis=1)
     ordered = jnp.dot(
         summed.reshape(-1, chan_total), pick.astype(F32), precision=lax.Precision.HIGHEST
     )

time: 485 us -> 455 us (0.938)
  Pallas kernels: 276 us -> 248 us
    ppermute x12 -> x11, waiting for transfers between devices: 47.5 us -> 25.6 us  [the longest x6 15.9 us: reduce_kept(): total = total + lax.ppermute(keep[step], 'dp', pairs)]
    ppermute x28, waiting for transfers between devices: 54.5 us -> 73.1 us  [send(): arrived[block] = lax.ppermute(blocks[block], 'ctx', pairs)]
    pallas_call x4, Pallas kernels: 200 us -> 182 us  [run_conv(): pl.pallas_call(functools.partial(conv_kernel, peers=peers, rows=rows, ori...]
    pallas_call x2, Pallas kernels: 18.7 us -> 13.2 us  [with_kernels(): pl.pallas_call(functools.partial(mixed_kernel, peers=peers, blocks=group)...]
    ppermute x12 -> x11, starting transfers between devices: 14.7 us -> 11.7 us  [the longest x6 8.9 us: reduce_kept(): total = total + lax.ppermute(keep[step], 'dp', pairs)]
  transfers between devices with their start and end apart: 41 -> 40, of which waited for: 14 -> 17; matrix products, arithmetic and copies ran while one was open for 0% -> 1% of each run, Pallas kernels for 52% -> 51%
where the time goes in v2:
time: 455 us; the launch traced here: 454 us
  Pallas kernels  248 us (55%)
  waiting for transfers between devices  98.7 us (22%)
  blocking collectives  43.6 us (10%)
  starting transfers between devices  40.3 us (9%)
  between operations  14.4 us (3%)
  local copies, waits for them, and re-layouts  5.53 us (1%)
    pallas_call x4, Pallas kernels, run_conv(): pl.pallas_call(functools.partial(conv_kernel, peers=peers, rows=rows, ori...  182 us
    ppermute x28, waiting for transfers between devices, send(): arrived[block] = lax.ppermute(blocks[block], 'ctx', pairs)  73.1 us
    all_to_all x1, blocking collectives, exchange(): lax.all_to_all(blocks, 'ctx', split_axis=0, concat_axis=0, tiled=True)  43.6 us
    ppermute x28, starting transfers between devices, send(): arrived[block] = lax.ppermute(blocks[block], 'ctx', pairs)  28.6 us
    pallas_call x1, Pallas kernels, with_kernels(): pl.pallas_call(smooth_kernel, grid=grid, in_specs=[POS_SPEC, tok_spec, to...  18 us
    ppermute x6, waiting for transfers between devices, reduce_kept(): total = total + lax.ppermute(keep[step], 'dp', pairs)  15.9 us
    pallas_call x2, Pallas kernels, with_kernels(): pl.pallas_call(functools.partial(mixed_kernel, peers=peers, blocks=group)...  13.2 us
    pallas_call x1, Pallas kernels, with_kernels(): pl.pallas_call(functools.partial(back_first_kernel, peers=peers, blocks=e...  12.6 us
  transfers between devices with their start and end apart: 40, of which 17 were waited for; matrix products, arithmetic and copies ran while one was open for 1% of the time, Pallas kernels for 51%

profile of v2, /device:TPU:0, one launch (start us, length us, event | category | flops | bytes accessed | tf_op | source)
XLA Modules:
  0.0 454.4 jit_solution(11346672370365821099)
XLA Ops:
  7.8 6.7 %mixed.2 = (bf16[2,32,16,512]{3,2,1,0:T(8,128)(2,1)}, bf16[2,32,16,512]{3,2,1,0:T(8,128)(2,1)}, bf16[2,32,16,512]{3,2,1,0:T(8,128)(2,1)}, bf16[2,32,16,512]{3,2,1,0:T(8,128)(2,1)}) custom-call(s32[2]{0:T(128)} %pad_add_fusion.pos_ref, bf16[16384,256]{1,0:T(8,128)(2,1)} %bitcast.73, bf16[256,768]{1,0:T(8,128)(2,1)} %w_ref.9, ...), custom_call_target="tpu_custom_call" | custom-call | flops 2147483648 | bytes 12582912 | tf_op jit(solution)/shard_map/mixed/pallas_call | solution.py:590
  14.5 2.9 collective-permute-start
  17.5 1.5 collective-permute-start.1
  19.0 1.1 fusion.2
  20.4 6.5 %mixed.3 = (bf16[2,32,16,512]{3,2,1,0:T(8,128)(2,1)}, bf16[2,32,16,512]{3,2,1,0:T(8,128)(2,1)}, bf16[2,32,16,512]{3,2,1,0:T(8,128)(2,1)}, bf16[2,32,16,512]{3,2,1,0:T(8,128)(2,1)}) custom-call(s32[2]{0:T(128)} %pad_add_fusion.pos_ref, bf16[16384,256]{1,0:T(8,128)(2,1)} %bitcast.74, bf16[256,768]{1,0:T(8,128)(2,1)} %w_ref.9, ...), custom_call_target="tpu_custom_call" | custom-call | flops 2147483648 | bytes 12582912 | tf_op jit(solution)/shard_map/mixed/pallas_call | solution.py:590
  26.9 43.6 %all_to_all.5 = bf16[8,2,2,16,512]{4,3,2,1,0:T(8,128)(2,1)} all-to-all(bf16[8,2,2,16,512]{4,3,2,1,0:T(8,128)(2,1)S(1)} %bitcast.83), channel_id=1, replica_groups=mesh['dp'=4,'ctx'=8] {'ctx'}, dimensions={0} | all-to-all | bytes 1048576 | tf_op jit(solution)/shard_map/all_to_all | solution.py:472
  70.6 1.1 collective-permute-start.6
  72.4 1.5 collective-permute-start.9
  73.9 11.7 %grad_smooth.1 = (bf16[2,32,16,512]{3,2,1,0:T(8,128)(2,1)}, bf16[2,32,16,512]{3,2,1,0:T(8,128)(2,1)}, bf16[2,32,16,512]{3,2,1,0:T(8,128)(2,1)}, bf16[2,32,16,512...) custom-call(s32[2]{0:T(128)} %pad_add_fusion.pos_ref, ...), custom_call_target="tpu_custom_call" | custom-call | flops 4294967296 | bytes 25165824 | tf_op jit(solution)/shard_map/grad_smooth/pallas_call | solution.py:612
  85.6 1.1 collective-permute-start.3
  86.7 9.4 %collective-permute-done.7 = bf16[2,32,16,512]{3,2,1,0:T(8,128)(2,1)S(1)} collective-permute-done((bf16[2,32,16,512]{3,2,1,0:T(8,128)(2,1)}, bf16[2,32,16,512]{3,2,1,0:T(8,128)(2,1)S(1)}, u32[]{:S(2)}, u32[]{:S(2)}) %collective-permute-start.7) | collective-permute-done | bytes 1048608 | tf_op jit(solution)/shard_map/ppermute | solution.py:467
  97.2 1.5 collective-permute-start.4
  100.6 19.1 %collective-permute-done.8 = bf16[2,32,16,512]{3,2,1,0:T(8,128)(2,1)} collective-permute-done((bf16[2,32,16,512]{3,2,1,0:T(8,128)(2,1)}, bf16[2,32,16,512]{3,2,1,0:T(8,128)(2,1)}, u32[]{:S(2)}, u32[]{:S(2)}) %collective-permute-start.8) | collective-permute-done | bytes 1048608 | tf_op jit(solution)/shard_map/ppermute | solution.py:467
  119.7 45.4 %conv.4 = (bf16[2,512,512]{2,1,0:T(8,128)(2,1)}, bf16[2,512,512]{2,1,0:T(8,128)(2,1)}, bf16[2,512,512]{2,1,0:T(8,128)(2,1)}, bf16[2,512,512]{2,1,0:T(8,128)(2,1)...) custom-call(s32[2]{0:T(128)} %pad_add_fusion.pos_ref, ...), custom_call_target="tpu_custom_call" | custom-call | flops 12884901888 | bytes 16777216 | tf_op jit(solution)/shard_map/conv/pallas_call | solution.py:291
  166.4 1.5 collective-permute-start.15
  168.6 45.3 %conv.5 = (bf16[2,512,512]{2,1,0:T(8,128)(2,1)}, bf16[2,512,512]{2,1,0:T(8,128)(2,1)}, bf16[2,512,512]{2,1,0:T(8,128)(2,1)}, bf16[2,512,512]{2,1,0:T(8,128)(2,1)...) custom-call(s32[2]{0:T(128)} %pad_add_fusion.pos_ref, ...), custom_call_target="tpu_custom_call", output_to_operand_aliasing={{0}: (16, {}), {1}: (17, {}), {2}: (18, {}), {3}: (19, {}),... | custom-call | flops 12884901888 | bytes 16777216 | tf_op jit(solution)/shard_map/conv/pallas_call | solution.py:291
  214.0 1.1 collective-permute-start.10
  215.1 1.5 collective-permute-start.11
  217.6 45.8 %conv.6 = (bf16[2,512,512]{2,1,0:T(8,128)(2,1)}, bf16[2,512,512]{2,1,0:T(8,128)(2,1)}, bf16[2,512,512]{2,1,0:T(8,128)(2,1)}, bf16[2,512,512]{2,1,0:T(8,128)(2,1)...) custom-call(s32[2]{0:T(128)} %pad_add_fusion.pos_ref, ...), custom_call_target="tpu_custom_call" | custom-call | flops 12884901888 | bytes 16777216 | tf_op jit(solution)/shard_map/conv/pallas_call | solution.py:291
  263.5 1.1 collective-permute-start.18
  264.7 1.2 collective-permute-start.19
  266.9 45.5 %conv.7 = (bf16[2,512,512]{2,1,0:T(8,128)(2,1)}, bf16[2,512,512]{2,1,0:T(8,128)(2,1)}, bf16[2,512,512]{2,1,0:T(8,128)(2,1)}, bf16[2,512,512]{2,1,0:T(8,128)(2,1)...) custom-call(s32[2]{0:T(128)} %pad_add_fusion.pos_ref, ...), custom_call_target="tpu_custom_call", output_to_operand_aliasing={{0}: (16, {}), {1}: (17, {}), {2}: (18, {}), {3}: (19, {}),... | custom-call | flops 12884901888 | bytes 16777216 | tf_op jit(solution)/shard_map/conv/pallas_call | solution.py:291
  312.4 1.1 collective-permute-start.21
  313.5 1.5 collective-permute-start.22
  315.9 18.0 %smooth.1 = (bf16[16384,256]{1,0:T(8,128)(2,1)}, f32[4,32,256]{2,1,0:T(8,128)}, f32[4,32,256]{2,1,0:T(8,128)}) custom-call(s32[2]{0:T(128)} %pad_add_fusion.pos_ref, bf16[16384,256]{1,0:T(8,128)(2,1)} %bitcast.76, bf16[16384,256]{1,0:T(8,128)(2,1)} %bitcast.80, bf16[256,768]{1,0:T(8,128)(2,1)} %w_ref.9, bf16[256,256]{1,0:T(8,128)(2,1)} %constant.48.clone.pick_ref, ...), custom_call_target="tpu_custom_call" | custom-call | flops 8589934592 | bytes 33554432 | tf_op jit(solution)/shard_map/smooth/pallas_call | solution.py:648
  333.9 4.7 %collective-permute-done.21 = bf16[2,512,512]{2,1,0:T(8,128)(2,1)S(1)} collective-permute-done((bf16[2,512,512]{2,1,0:T(8,128)(2,1)}, bf16[2,512,512]{2,1,0:T(8,128)(2,1)S(1)}, u32[]{:S(2)}, u32[]{:S(2)}) %collective-permute-start.21) | collective-permute-done | bytes 1048608 | tf_op jit(solution)/shard_map/ppermute | solution.py:467
  338.7 22.3 %collective-permute-done.22 = bf16[2,512,512]{2,1,0:T(8,128)(2,1)S(1)} collective-permute-done((bf16[2,512,512]{2,1,0:T(8,128)(2,1)}, bf16[2,512,512]{2,1,0:T(8,128)(2,1)S(1)}, u32[]{:S(2)}, u32[]{:S(2)}) %collective-permute-start.22) | collective-permute-done | bytes 1048608 | tf_op jit(solution)/shard_map/ppermute | solution.py:467
  362.4 1.8 collective-permute-start.29
  364.2 1.2 collective-permute-start.30
  366.6 1.6 collective-permute-start.25
  368.3 4.1 collective-permute-done.25
  372.4 1.8 collective-permute-start.27
  374.2 2.1 collective-permute-done.27
  377.1 4.0 collective-permute-done.26
  381.1 12.6 %back_first.1 = (f32[256,512]{1,0:T(8,128)}, bf16[320,16384]{1,0:T(8,128)(2,1)}) custom-call(s32[2]{0:T(128)} %pad_add_fusion.pos_ref, bf16[16384,256]{1,0:T(8,128)(2,1)} %bitcast.77, bf16[256,768]{1,0:T(8,128)(2,1)} %w_ref.9, bf16[256,256]{1,0:T(8,128)(2,1)} %constant.48.clone.pick_ref, bf16[2,32,16,512]{3,2,1,0:T(8,128)(2,1)} %bitcast.104, ...), custom_call_target="tpu_custom_call" | custom-call | flops 6442450944 | bytes 25165824 | tf_op jit(solution)/shard_map/back_first/pallas_call | solution.py:669
  393.8 16.2 %collective-permute-done.29 = bf16[2,512,512]{2,1,0:T(8,128)(2,1)S(1)} collective-permute-done((bf16[2,512,512]{2,1,0:T(8,128)(2,1)}, bf16[2,512,512]{2,1,0:T(8,128)(2,1)S(1)}, u32[]{:S(2)}, u32[]{:S(2)}) %collective-permute-start.29) | collective-permute-done | bytes 1048608 | tf_op jit(solution)/shard_map/ppermute | solution.py:467
  410.0 1.2 collective-permute-done.30
  412.2 10.3 %back_last.1 = (f32[4,32,512]{2,1,0:T(8,128)}, f32[4,32,512]{2,1,0:T(8,128)}) custom-call(s32[2]{0:T(128)} %pad_add_fusion.pos_ref, bf16[16384,256]{1,0:T(8,128)(2,1)} %bitcast.78, bf16[320,16384]{1,0:T(8,128)(2,1)} %get-tuple-element.265.feat_ref, f32[256,512]{1,0:T(8,128)} %get-tuple-element.266.earlier_ref, bf16[2,32,16,512]{3,2,1,0:T(8,128)(2,1)} %bitcast.84, ...), custom_call_target="tpu_custom_call" | custom-call | flops 2147483648 | bytes 20971520 | tf_op jit(solution)/shard_map/back_last/pallas_call | solution.py:687
  422.8 1.6 collective-permute-done.32
  425.4 1.6 collective-permute-start.33
  427.0 2.2 collective-permute-start.35
  430.1 1.6 collective-permute-done.33
  432.3 3.4 collective-permute-done.34
  435.7 1.2 collective-permute-start.36
  436.9 3.5 collective-permute-done.36
  440.4 1.3 collective-permute-start.37
  441.8 3.4 collective-permute-done.37
  445.2 1.3 collective-permute-done.38
  (95 shorter events, 18.0 us)
Async XLA Ops:
  7.2 112.6 %all-gather.3.cloned.1.call-start = ((), (), s32[]{:S(2)}) async-start(), calls=%async_computation.1 | async-start | bytes 2621440 | tf_op jit(solution)/shard_map/all_gather | solution.py:623
  14.5 56.0 %collective-permute-start = (bf16[2,32,16,512]{3,2,1,0:T(8,128)(2,1)}, bf16[2,32,16,512]{3,2,1,0:T(8,128)(2,1)S(1)}, u32[]{:S(2)}, u32[]{:S(2)}) collective-permute-start(bf16[2,32,16,512]{3,2,1,0:T(8,128)(2,1)} %get-tuple-element.150), channel_id=1, source_target_pairs={{0,2},{1,3},{2,0},{3,1},{4,6},{5,7},{6,4},{7,5},{8,10},{9,11},{10,... | collective-permute-start | bytes 3145736 | tf_op jit(solution)/shard_map/ppermute | solution.py:467
  17.5 53.0 %collective-permute-start.1 = (bf16[2,32,16,512]{3,2,1,0:T(8,128)(2,1)}, bf16[2,32,16,512]{3,2,1,0:T(8,128)(2,1)}, u32[]{:S(2)}, u32[]{:S(2)}) collective-permute-start(bf16[2,32,16,512]{3,2,1,0:T(8,128)(2,1)} %get-tuple-element.151), channel_id=1, source_target_pairs={{0,4},{1,5},{2,6},{3,7},{4,0},{5,1},{6,2},{7,3},{8,12},{9,13},{10,... | collective-permute-start | bytes 3145736 | tf_op jit(solution)/shard_map/ppermute | solution.py:467
  19.0 51.5 %collective-permute-start.2 = (bf16[2,32,16,512]{3,2,1,0:T(8,128)(2,1)}, bf16[2,32,16,512]{3,2,1,0:T(8,128)(2,1)}, u32[]{:S(2)}, u32[]{:S(2)}) collective-permute-start(bf16[2,32,16,512]{3,2,1,0:T(8,128)(2,1)} %get-tuple-element.152), channel_id=1, source_target_pairs={{0,6},{1,7},{2,4},{3,5},{4,2},{5,3},{6,0},{7,1},{8,14},{9,15},{10,... | collective-permute-start | bytes 3145736 | tf_op jit(solution)/shard_map/ppermute | solution.py:467
  70.5 25.7 %collective-permute-start.7 = (bf16[2,32,16,512]{3,2,1,0:T(8,128)(2,1)}, bf16[2,32,16,512]{3,2,1,0:T(8,128)(2,1)S(1)}, u32[]{:S(2)}, u32[]{:S(2)}) collective-permute-start(bf16[2,32,16,512]{3,2,1,0:T(8,128)(2,1)} %get-tuple-element.165), channel_id=1, source_target_pairs={{0,3},{1,2},{2,1},{3,0},{4,7},{5,6},{6,5},{7,4},{8,11},{9,10},{10,... | collective-permute-start | bytes 3145736 | tf_op jit(solution)/shard_map/ppermute | solution.py:467
  70.6 28.1 %collective-permute-start.6 = (bf16[2,32,16,512]{3,2,1,0:T(8,128)(2,1)}, bf16[2,32,16,512]{3,2,1,0:T(8,128)(2,1)S(1)}, u32[]{:S(2)}, u32[]{:S(2)}) collective-permute-start(bf16[2,32,16,512]{3,2,1,0:T(8,128)(2,1)} %get-tuple-element.163), channel_id=1, source_target_pairs={{0,1},{1,0},{2,3},{3,2},{4,5},{5,4},{6,7},{7,6},{8,9},{9,8},{10,11... | collective-permute-start | bytes 3145736 | tf_op jit(solution)/shard_map/ppermute | solution.py:467
  71.7 48.0 %collective-permute-start.8 = (bf16[2,32,16,512]{3,2,1,0:T(8,128)(2,1)}, bf16[2,32,16,512]{3,2,1,0:T(8,128)(2,1)}, u32[]{:S(2)}, u32[]{:S(2)}) collective-permute-start(bf16[2,32,16,512]{3,2,1,0:T(8,128)(2,1)} %get-tuple-element.167), channel_id=1, source_target_pairs={{0,5},{1,4},{2,7},{3,6},{4,1},{5,0},{6,3},{7,2},{8,13},{9,12},{10,... | collective-permute-start | bytes 3145736 | tf_op jit(solution)/shard_map/ppermute | solution.py:467
  72.4 47.4 %collective-permute-start.9 = (bf16[2,32,16,512]{3,2,1,0:T(8,128)(2,1)}, bf16[2,32,16,512]{3,2,1,0:T(8,128)(2,1)}, u32[]{:S(2)}, u32[]{:S(2)}) collective-permute-start(bf16[2,32,16,512]{3,2,1,0:T(8,128)(2,1)} %get-tuple-element.169), channel_id=1, source_target_pairs={{0,7},{1,6},{2,5},{3,4},{4,3},{5,2},{6,1},{7,0},{8,15},{9,14},{10,... | collective-permute-start | bytes 3145736 | tf_op jit(solution)/shard_map/ppermute | solution.py:467
  85.6 79.5 %collective-permute-start.3 = (bf16[2,512,512]{2,1,0:T(8,128)(2,1)}, bf16[2,512,512]{2,1,0:T(8,128)(2,1)S(1)}, u32[]{:S(2)}, u32[]{:S(2)}) collective-permute-start(bf16[2,512,512]{2,1,0:T(8,128)(2,1)} %bitcast.114), channel_id=1, source_target_pairs={{0,2},{1,3},{2,0},{3,1},{4,6},{5,7},{6,4},{7,5},{8,10},{9,11},{10,... | collective-permute-start | bytes 3145736 | tf_op jit(solution)/shard_map/ppermute | solution.py:467
  97.2 67.9 %collective-permute-start.4 = (bf16[2,512,512]{2,1,0:T(8,128)(2,1)}, bf16[2,512,512]{2,1,0:T(8,128)(2,1)S(1)}, u32[]{:S(2)}, u32[]{:S(2)}) collective-permute-start(bf16[2,512,512]{2,1,0:T(8,128)(2,1)} %bitcast.113), channel_id=1, source_target_pairs={{0,4},{1,5},{2,6},{3,7},{4,0},{5,1},{6,2},{7,3},{8,12},{9,13},{10,... | collective-permute-start | bytes 3145736 | tf_op jit(solution)/shard_map/ppermute | solution.py:467
  99.7 65.5 %collective-permute-start.5 = (bf16[2,512,512]{2,1,0:T(8,128)(2,1)}, bf16[2,512,512]{2,1,0:T(8,128)(2,1)S(1)}, u32[]{:S(2)}, u32[]{:S(2)}) collective-permute-start(bf16[2,512,512]{2,1,0:T(8,128)(2,1)} %bitcast.112), channel_id=1, source_target_pairs={{0,6},{1,7},{2,4},{3,5},{4,2},{5,3},{6,0},{7,1},{8,14},{9,15},{10,... | collective-permute-start | bytes 3145736 | tf_op jit(solution)/shard_map/ppermute | solution.py:467
  165.2 48.8 %copy-start.5 = (bf16[2,512,512]{2,1,0:T(8,128)(2,1)}, bf16[2,512,512]{2,1,0:T(8,128)(2,1)S(1)}, u32[]{:S(2)}) copy-start(bf16[2,512,512]{2,1,0:T(8,128)(2,1)S(1)} %collective-permute-done.3.args_2_) | copy-start | bytes 3145732
  165.2 48.8 %copy-start.6 = (bf16[2,512,512]{2,1,0:T(8,128)(2,1)}, bf16[2,512,512]{2,1,0:T(8,128)(2,1)S(1)}, u32[]{:S(2)}) copy-start(bf16[2,512,512]{2,1,0:T(8,128)(2,1)S(1)} %collective-permute-done.4.args_4_) | copy-start | bytes 3145732
  165.2 48.8 %copy-start.7 = (bf16[2,512,512]{2,1,0:T(8,128)(2,1)}, bf16[2,512,512]{2,1,0:T(8,128)(2,1)S(1)}, u32[]{:S(2)}) copy-start(bf16[2,512,512]{2,1,0:T(8,128)(2,1)S(1)} %collective-permute-done.5.args_6_) | copy-start | bytes 3145732
  165.2 49.9 %collective-permute-start.13 = (bf16[2,512,512]{2,1,0:T(8,128)(2,1)}, bf16[2,512,512]{2,1,0:T(8,128)(2,1)}, u32[]{:S(2)}, u32[]{:S(2)}) collective-permute-start(bf16[2,512,512]{2,1,0:T(8,128)(2,1)} %bitcast.107), channel_id=1, source_target_pairs={{0,1},{1,0},{2,3},{3,2},{4,5},{5,4},{6,7},{7,6},{8,9},{9,8},{10,11... | collective-permute-start | bytes 3145736 | tf_op jit(solution)/shard_map/ppermute | solution.py:467
  165.6 51.0 %collective-permute-start.14 = (bf16[2,512,512]{2,1,0:T(8,128)(2,1)}, bf16[2,512,512]{2,1,0:T(8,128)(2,1)}, u32[]{:S(2)}, u32[]{:S(2)}) collective-permute-start(bf16[2,512,512]{2,1,0:T(8,128)(2,1)} %bitcast.103), channel_id=1, source_target_pairs={{0,3},{1,2},{2,1},{3,0},{4,7},{5,6},{6,5},{7,4},{8,11},{9,10},{10,... | collective-permute-start | bytes 3145736 | tf_op jit(solution)/shard_map/ppermute | solution.py:467
  166.4 51.1 %collective-permute-start.15 = (bf16[2,512,512]{2,1,0:T(8,128)(2,1)}, bf16[2,512,512]{2,1,0:T(8,128)(2,1)}, u32[]{:S(2)}, u32[]{:S(2)}) collective-permute-start(bf16[2,512,512]{2,1,0:T(8,128)(2,1)} %bitcast.101), channel_id=1, source_target_pairs={{0,5},{1,4},{2,7},{3,6},{4,1},{5,0},{6,3},{7,2},{8,13},{9,12},{10,... | collective-permute-start | bytes 3145736 | tf_op jit(solution)/shard_map/ppermute | solution.py:467
  167.9 49.6 %collective-permute-start.16 = (bf16[2,512,512]{2,1,0:T(8,128)(2,1)}, bf16[2,512,512]{2,1,0:T(8,128)(2,1)}, u32[]{:S(2)}, u32[]{:S(2)}) collective-permute-start(bf16[2,512,512]{2,1,0:T(8,128)(2,1)} %bitcast.99), channel_id=1, source_target_pairs={{0,7},{1,6},{2,5},{3,4},{4,3},{5,2},{6,1},{7,0},{8,15},{9,14},{10,... | collective-permute-start | bytes 3145736 | tf_op jit(solution)/shard_map/ppermute | solution.py:467
  214.0 49.4 %collective-permute-start.10 = (bf16[2,512,512]{2,1,0:T(8,128)(2,1)}, bf16[2,512,512]{2,1,0:T(8,128)(2,1)S(1)}, u32[]{:S(2)}, u32[]{:S(2)}) collective-permute-start(bf16[2,512,512]{2,1,0:T(8,128)(2,1)} %get-tuple-element.198), channel_id=1, source_target_pairs={{0,2},{1,3},{2,0},{3,1},{4,6},{5,7},{6,4},{7,5},{8,10},{9,11},{10,... | collective-permute-start | bytes 3145736 | tf_op jit(solution)/shard_map/ppermute | solution.py:467
  215.1 48.3 %collective-permute-start.11 = (bf16[2,512,512]{2,1,0:T(8,128)(2,1)}, bf16[2,512,512]{2,1,0:T(8,128)(2,1)S(1)}, u32[]{:S(2)}, u32[]{:S(2)}) collective-permute-start(bf16[2,512,512]{2,1,0:T(8,128)(2,1)} %get-tuple-element.200), channel_id=1, source_target_pairs={{0,4},{1,5},{2,6},{3,7},{4,0},{5,1},{6,2},{7,3},{8,12},{9,13},{10,... | collective-permute-start | bytes 3145736 | tf_op jit(solution)/shard_map/ppermute | solution.py:467
  216.6 46.8 %collective-permute-start.12 = (bf16[2,512,512]{2,1,0:T(8,128)(2,1)}, bf16[2,512,512]{2,1,0:T(8,128)(2,1)S(1)}, u32[]{:S(2)}, u32[]{:S(2)}) collective-permute-start(bf16[2,512,512]{2,1,0:T(8,128)(2,1)} %get-tuple-element.202), channel_id=1, source_target_pairs={{0,6},{1,7},{2,4},{3,5},{4,2},{5,3},{6,0},{7,1},{8,14},{9,15},{10,... | collective-permute-start | bytes 3145736 | tf_op jit(solution)/shard_map/ppermute | solution.py:467
  263.4 49.0 %copy-start.9 = (bf16[2,512,512]{2,1,0:T(8,128)(2,1)}, bf16[2,512,512]{2,1,0:T(8,128)(2,1)S(1)}, u32[]{:S(2)}) copy-start(bf16[2,512,512]{2,1,0:T(8,128)(2,1)S(1)} %collective-permute-done.10) | copy-start | bytes 3145732
  263.4 48.9 %copy-start.10 = (bf16[2,512,512]{2,1,0:T(8,128)(2,1)}, bf16[2,512,512]{2,1,0:T(8,128)(2,1)S(1)}, u32[]{:S(2)}) copy-start(bf16[2,512,512]{2,1,0:T(8,128)(2,1)S(1)} %collective-permute-done.11) | copy-start | bytes 3145732
  263.4 48.9 %copy-start.11 = (bf16[2,512,512]{2,1,0:T(8,128)(2,1)}, bf16[2,512,512]{2,1,0:T(8,128)(2,1)S(1)}, u32[]{:S(2)}) copy-start(bf16[2,512,512]{2,1,0:T(8,128)(2,1)S(1)} %collective-permute-done.12) | copy-start | bytes 3145732
  263.4 50.0 %collective-permute-start.17 = (bf16[2,512,512]{2,1,0:T(8,128)(2,1)}, bf16[2,512,512]{2,1,0:T(8,128)(2,1)}, u32[]{:S(2)}, u32[]{:S(2)}) collective-permute-start(bf16[2,512,512]{2,1,0:T(8,128)(2,1)} %get-tuple-element.240), channel_id=1, source_target_pairs={{0,1},{1,0},{2,3},{3,2},{4,5},{5,4},{6,7},{7,6},{8,9},{9,8},{10,11... | collective-permute-start | bytes 3145736 | tf_op jit(solution)/shard_map/ppermute | solution.py:467
  263.5 51.4 %collective-permute-start.18 = (bf16[2,512,512]{2,1,0:T(8,128)(2,1)}, bf16[2,512,512]{2,1,0:T(8,128)(2,1)}, u32[]{:S(2)}, u32[]{:S(2)}) collective-permute-start(bf16[2,512,512]{2,1,0:T(8,128)(2,1)} %get-tuple-element.242), channel_id=1, source_target_pairs={{0,3},{1,2},{2,1},{3,0},{4,7},{5,6},{6,5},{7,4},{8,11},{9,10},{10,... | collective-permute-start | bytes 3145736 | tf_op jit(solution)/shard_map/ppermute | solution.py:467
  264.7 51.3 %collective-permute-start.19 = (bf16[2,512,512]{2,1,0:T(8,128)(2,1)}, bf16[2,512,512]{2,1,0:T(8,128)(2,1)}, u32[]{:S(2)}, u32[]{:S(2)}) collective-permute-start(bf16[2,512,512]{2,1,0:T(8,128)(2,1)} %get-tuple-element.244), channel_id=1, source_target_pairs={{0,5},{1,4},{2,7},{3,6},{4,1},{5,0},{6,3},{7,2},{8,13},{9,12},{10,... | collective-permute-start | bytes 3145736 | tf_op jit(solution)/shard_map/ppermute | solution.py:467
  265.8 50.1 %collective-permute-start.20 = (bf16[2,512,512]{2,1,0:T(8,128)(2,1)}, bf16[2,512,512]{2,1,0:T(8,128)(2,1)}, u32[]{:S(2)}, u32[]{:S(2)}) collective-permute-start(bf16[2,512,512]{2,1,0:T(8,128)(2,1)} %get-tuple-element.246), channel_id=1, source_target_pairs={{0,7},{1,6},{2,5},{3,4},{4,3},{5,2},{6,1},{7,0},{8,15},{9,14},{10,... | collective-permute-start | bytes 3145736 | tf_op jit(solution)/shard_map/ppermute | solution.py:467
  312.4 26.3 %collective-permute-start.21 = (bf16[2,512,512]{2,1,0:T(8,128)(2,1)}, bf16[2,512,512]{2,1,0:T(8,128)(2,1)S(1)}, u32[]{:S(2)}, u32[]{:S(2)}) collective-permute-start(bf16[2,512,512]{2,1,0:T(8,128)(2,1)} %get-tuple-element.250), channel_id=1, source_target_pairs={{0,2},{1,3},{2,0},{3,1},{4,6},{5,7},{6,4},{7,5},{8,10},{9,11},{10,... | collective-permute-start | bytes 3145736 | tf_op jit(solution)/shard_map/ppermute | solution.py:467
  313.5 47.5 %collective-permute-start.22 = (bf16[2,512,512]{2,1,0:T(8,128)(2,1)}, bf16[2,512,512]{2,1,0:T(8,128)(2,1)S(1)}, u32[]{:S(2)}, u32[]{:S(2)}) collective-permute-start(bf16[2,512,512]{2,1,0:T(8,128)(2,1)} %get-tuple-element.252), channel_id=1, source_target_pairs={{0,4},{1,5},{2,6},{3,7},{4,0},{5,1},{6,2},{7,3},{8,12},{9,13},{10,... | collective-permute-start | bytes 3145736 | tf_op jit(solution)/shard_map/ppermute | solution.py:467
  315.0 46.0 %collective-permute-start.23 = (bf16[2,512,512]{2,1,0:T(8,128)(2,1)}, bf16[2,512,512]{2,1,0:T(8,128)(2,1)S(1)}, u32[]{:S(2)}, u32[]{:S(2)}) collective-permute-start(bf16[2,512,512]{2,1,0:T(8,128)(2,1)} %get-tuple-element.254), channel_id=1, source_target_pairs={{0,6},{1,7},{2,4},{3,5},{4,2},{5,3},{6,0},{7,1},{8,14},{9,15},{10,... | collective-permute-start | bytes 3145736 | tf_op jit(solution)/shard_map/ppermute | solution.py:467
  338.7 22.3 %copy-start.12 = (bf16[2,512,512]{2,1,0:T(8,128)(2,1)}, bf16[2,512,512]{2,1,0:T(8,128)(2,1)S(1)}, u32[]{:S(2)}) copy-start(bf16[2,512,512]{2,1,0:T(8,128)(2,1)S(1)} %collective-permute-done.21) | copy-start | bytes 3145732
  362.0 3.7 collective-permute-start.24
  362.3 31.4 %collective-permute-start.28 = (bf16[2,512,512]{2,1,0:T(8,128)(2,1)}, bf16[2,512,512]{2,1,0:T(8,128)(2,1)S(1)}, u32[]{:S(2)}, u32[]{:S(2)}) collective-permute-start(bf16[2,512,512]{2,1,0:T(8,128)(2,1)} %get-tuple-element.267), channel_id=1, source_target_pairs={{0,3},{1,2},{2,1},{3,0},{4,7},{5,6},{6,5},{7,4},{8,11},{9,10},{10,... | collective-permute-start | bytes 3145736 | tf_op jit(solution)/shard_map/ppermute | solution.py:467
  362.4 47.6 %collective-permute-start.29 = (bf16[2,512,512]{2,1,0:T(8,128)(2,1)}, bf16[2,512,512]{2,1,0:T(8,128)(2,1)S(1)}, u32[]{:S(2)}, u32[]{:S(2)}) collective-permute-start(bf16[2,512,512]{2,1,0:T(8,128)(2,1)} %get-tuple-element.268), channel_id=1, source_target_pairs={{0,5},{1,4},{2,7},{3,6},{4,1},{5,0},{6,3},{7,2},{8,13},{9,12},{10,... | collective-permute-start | bytes 3145736 | tf_op jit(solution)/shard_map/ppermute | solution.py:467
  364.2 47.0 %collective-permute-start.30 = (bf16[2,512,512]{2,1,0:T(8,128)(2,1)}, bf16[2,512,512]{2,1,0:T(8,128)(2,1)S(1)}, u32[]{:S(2)}, u32[]{:S(2)}) collective-permute-start(bf16[2,512,512]{2,1,0:T(8,128)(2,1)} %get-tuple-element.269), channel_id=1, source_target_pairs={{0,7},{1,6},{2,5},{3,4},{4,3},{5,2},{6,1},{7,0},{8,15},{9,14},{10,... | collective-permute-start | bytes 3145736 | tf_op jit(solution)/shard_map/ppermute | solution.py:467
  365.3 45.9 %collective-permute-start.31 = (bf16[2,512,512]{2,1,0:T(8,128)(2,1)}, bf16[2,512,512]{2,1,0:T(8,128)(2,1)}, u32[]{:S(2)}, u32[]{:S(2)}) collective-permute-start(bf16[2,512,512]{2,1,0:T(8,128)(2,1)} %get-tuple-element.270), channel_id=1, source_target_pairs={{0,1},{1,0},{2,3},{3,2},{4,5},{5,4},{6,7},{7,6},{8,9},{9,8},{10,11... | collective-permute-start | bytes 3145736 | tf_op jit(solution)/shard_map/ppermute | solution.py:467
  366.6 5.8 %collective-permute-start.25 = (f32[32,256]{1,0:T(8,128)S(1)}, f32[32,256]{1,0:T(8,128)S(1)}, u32[]{:S(2)}, u32[]{:S(2)}) collective-permute-start(f32[32,256]{1,0:T(8,128)S(1)} %get-tuple-element.279), channel_id=1, source_target_pairs={{0,8},{8,16},{16,24},{24,0},{1,9},{9,17},{17,25},{25,1},{2,10},{10... | collective-permute-start | bytes 98312 | tf_op jit(solution)/shard_map/ppermute | solution.py:528
  372.4 3.9 collective-permute-start.27
  376.3 4.8 %collective-permute-start.26 = (f32[32,256]{1,0:T(8,128)S(1)}, f32[32,256]{1,0:T(8,128)S(1)}, u32[]{:S(2)}, u32[]{:S(2)}) collective-permute-start(f32[32,256]{1,0:T(8,128)S(1)} %get-tuple-element.281), channel_id=1, source_target_pairs={{0,16},{8,24},{16,0},{24,8},{1,17},{9,25},{17,1},{25,9},{2,18},{10... | collective-permute-start | bytes 98312 | tf_op jit(solution)/shard_map/ppermute | solution.py:528
  422.6 24.0 %copy-start = (bf16[256,256]{1,0:T(8,128)(2,1)S(1)}, bf16[256,256]{1,0:T(8,128)(2,1)}, u32[]{:S(2)}) copy-start(bf16[256,256]{1,0:T(8,128)(2,1)} %constant.48.clone.pick_ref) | copy-start | bytes 393220
  422.6 1.8 collective-permute-start.32
  425.4 6.2 %collective-permute-start.33 = (f32[32,512]{1,0:T(8,128)S(1)}, f32[32,512]{1,0:T(8,128)S(1)}, u32[]{:S(2)}, u32[]{:S(2)}) collective-permute-start(f32[32,512]{1,0:T(8,128)S(1)} %get-tuple-element.274), channel_id=1, source_target_pairs={{0,8},{8,16},{16,24},{24,0},{1,9},{9,17},{17,25},{25,1},{2,10},{10... | collective-permute-start | bytes 196616 | tf_op jit(solution)/shard_map/ppermute | solution.py:528
  427.0 5.3 %collective-permute-start.35 = (f32[32,512]{1,0:T(8,128)S(1)}, f32[32,512]{1,0:T(8,128)S(1)}, u32[]{:S(2)}, u32[]{:S(2)}) collective-permute-start(f32[32,512]{1,0:T(8,128)S(1)} %get-tuple-element.275), channel_id=1, source_target_pairs={{0,24},{8,0},{16,8},{24,16},{1,25},{9,1},{17,9},{25,17},{2,26},{10... | collective-permute-start | bytes 196616 | tf_op jit(solution)/shard_map/ppermute | solution.py:528
  429.3 6.4 %collective-permute-start.34 = (f32[32,512]{1,0:T(8,128)S(1)}, f32[32,512]{1,0:T(8,128)S(1)}, u32[]{:S(2)}, u32[]{:S(2)}) collective-permute-start(f32[32,512]{1,0:T(8,128)S(1)} %get-tuple-element.276), channel_id=1, source_target_pairs={{0,16},{8,24},{16,0},{24,8},{1,17},{9,25},{17,1},{25,9},{2,18},{10... | collective-permute-start | bytes 196616 | tf_op jit(solution)/shard_map/ppermute | solution.py:528
  435.7 4.7 %collective-permute-start.36 = (f32[32,768]{1,0:T(8,128)S(1)}, f32[32,768]{1,0:T(8,128)S(1)}, u32[]{:S(2)}, u32[]{:S(2)}) collective-permute-start(f32[32,768]{1,0:T(8,128)S(1)} %pad_maximum_fusion.1), channel_id=1, source_target_pairs={{0,2},{1,3},{2,0},{3,1},{4,6},{5,7},{6,4},{7,5},{8,10},{9,11},{10,... | collective-permute-start | bytes 294920 | tf_op jit(solution)/shard_map/ppermute | solution.py:519
  440.4 4.7 %collective-permute-start.37 = (f32[32,768]{1,0:T(8,128)S(1)}, f32[32,768]{1,0:T(8,128)S(1)}, u32[]{:S(2)}, u32[]{:S(2)}) collective-permute-start(f32[32,768]{1,0:T(8,128)S(1)} %fusion.9), channel_id=1, source_target_pairs={{0,4},{1,5},{2,6},{3,7},{4,0},{5,1},{6,2},{7,3},{8,12},{9,13},{10,... | collective-permute-start | bytes 294920 | tf_op jit(solution)/shard_map/ppermute | solution.py:519
  445.1 1.4 collective-permute-start.38
  (9 other events, 50.3 us)
Sparse Core Ops, SparseCore 0:
  70.6 46.2 all-gather.2

commit v3 on v2

--- a/solution.py
+++ b/solution.py
@@ -530,10 +530,10 @@
 
 
 def reduce_chips(total):
-    step = 2
-    while step < lax.axis_size("ctx"):
-        total = total + swap(total, step)
-        step *= 2
+    terms = [total] + [swap(total, step) for step in range(2, lax.axis_size("ctx"), 2)]
+    while len(terms) > 1:
+        terms = [left + right for left, right in zip(terms[::2], terms[1::2])]
+    total = terms[0]
     other = swap(total, 1)
     upper = lax.axis_index("ctx") % 2 != 0
     return jnp.concatenate([jnp.where(upper, other, total), jnp.where(upper, total, other)])
@@ -636,6 +636,7 @@
     back = conv(grads, 1, -1.0, last, back)
     smooth = send(smooth, late)
     last, back = after(back, pos)
+    early, late = early + (1, 0), late[:-2]
     back = send(back, early)
 
     def kept(cols):

time: 455 us -> 451 us (level)
    ppermute x5 -> x6, waiting for transfers between devices: 9.75 us -> 7.51 us  [swap(): return lax.ppermute(value, 'ctx', pairs)]
  transfers between devices with their start and end apart: 40 -> 41, of which waited for: 17 -> 18; matrix products, arithmetic and copies ran while one was open for 1% -> 1% of each run, Pallas kernels for 51% -> 51%
where the time goes in v3:
time: 451 us
  Pallas kernels  247 us (55%)
  waiting for transfers between devices  96.4 us (21%)
  blocking collectives  43.6 us (10%)
  starting transfers between devices  41.7 us (9%)
  between operations  14.4 us (3%)
    pallas_call x4, Pallas kernels, run_conv(): pl.pallas_call(functools.partial(conv_kernel, peers=peers, rows=rows, ori...  182 us
    ppermute x28, waiting for transfers between devices, send(): arrived[block] = lax.ppermute(blocks[block], 'ctx', pairs)  77.1 us
    all_to_all x1, blocking collectives, exchange(): lax.all_to_all(blocks, 'ctx', split_axis=0, concat_axis=0, tiled=True)  43.6 us
    ppermute x28, starting transfers between devices, send(): arrived[block] = lax.ppermute(blocks[block], 'ctx', pairs)  28.9 us
    pallas_call x1, Pallas kernels, with_kernels(): pl.pallas_call(smooth_kernel, grid=grid, in_specs=[POS_SPEC, tok_spec, to...  18 us
    pallas_call x1, Pallas kernels, with_kernels(): pl.pallas_call(functools.partial(back_first_kernel, peers=peers, blocks=e...  13.5 us
    pallas_call x2, Pallas kernels, with_kernels(): pl.pallas_call(functools.partial(mixed_kernel, peers=peers, blocks=group)...  13.2 us
    ppermute x6, waiting for transfers between devices, reduce_kept(): total = total + lax.ppermute(keep[step], 'dp', pairs)  11.8 us
  transfers between devices with their start and end apart: 41, of which 18 were waited for; matrix products, arithmetic and copies ran while one was open for 1% of the time, Pallas kernels for 51%

profile of v3, /device:TPU:0, one launch (start us, length us, event | category | flops | bytes accessed | tf_op | source)
XLA Modules:
  0.0 451.0 jit_solution(2852439958709055668)
XLA Ops:
  7.8 6.7 %mixed.2 = (bf16[2,32,16,512]{3,2,1,0:T(8,128)(2,1)}, bf16[2,32,16,512]{3,2,1,0:T(8,128)(2,1)}, bf16[2,32,16,512]{3,2,1,0:T(8,128)(2,1)}, bf16[2,32,16,512]{3,2,1,0:T(8,128)(2,1)}) custom-call(s32[2]{0:T(128)} %pad_add_fusion.pos_ref, bf16[16384,256]{1,0:T(8,128)(2,1)} %bitcast.73, bf16[256,768]{1,0:T(8,128)(2,1)} %w_ref.9, ...), custom_call_target="tpu_custom_call" | custom-call | flops 2147483648 | bytes 12582912 | tf_op jit(solution)/shard_map/mixed/pallas_call | solution.py:590
  14.5 2.9 collective-permute-start
  17.4 1.5 collective-permute-start.1
  19.0 1.1 fusion.2
  20.4 6.5 %mixed.3 = (bf16[2,32,16,512]{3,2,1,0:T(8,128)(2,1)}, bf16[2,32,16,512]{3,2,1,0:T(8,128)(2,1)}, bf16[2,32,16,512]{3,2,1,0:T(8,128)(2,1)}, bf16[2,32,16,512]{3,2,1,0:T(8,128)(2,1)}) custom-call(s32[2]{0:T(128)} %pad_add_fusion.pos_ref, bf16[16384,256]{1,0:T(8,128)(2,1)} %bitcast.74, bf16[256,768]{1,0:T(8,128)(2,1)} %w_ref.9, ...), custom_call_target="tpu_custom_call" | custom-call | flops 2147483648 | bytes 12582912 | tf_op jit(solution)/shard_map/mixed/pallas_call | solution.py:590
  26.9 43.6 %all_to_all.5 = bf16[8,2,2,16,512]{4,3,2,1,0:T(8,128)(2,1)} all-to-all(bf16[8,2,2,16,512]{4,3,2,1,0:T(8,128)(2,1)S(1)} %bitcast.83), channel_id=1, replica_groups=mesh['dp'=4,'ctx'=8] {'ctx'}, dimensions={0} | all-to-all | bytes 1048576 | tf_op jit(solution)/shard_map/all_to_all | solution.py:472
  70.6 1.0 collective-permute-start.6
  72.3 1.5 collective-permute-start.9
  73.9 11.7 %grad_smooth.1 = (bf16[2,32,16,512]{3,2,1,0:T(8,128)(2,1)}, bf16[2,32,16,512]{3,2,1,0:T(8,128)(2,1)}, bf16[2,32,16,512]{3,2,1,0:T(8,128)(2,1)}, bf16[2,32,16,512...) custom-call(s32[2]{0:T(128)} %pad_add_fusion.pos_ref, ...), custom_call_target="tpu_custom_call" | custom-call | flops 4294967296 | bytes 25165824 | tf_op jit(solution)/shard_map/grad_smooth/pallas_call | solution.py:612
  85.6 1.1 collective-permute-start.3
  86.7 9.4 %collective-permute-done.7 = bf16[2,32,16,512]{3,2,1,0:T(8,128)(2,1)S(1)} collective-permute-done((bf16[2,32,16,512]{3,2,1,0:T(8,128)(2,1)}, bf16[2,32,16,512]{3,2,1,0:T(8,128)(2,1)S(1)}, u32[]{:S(2)}, u32[]{:S(2)}) %collective-permute-start.7) | collective-permute-done | bytes 1048608 | tf_op jit(solution)/shard_map/ppermute | solution.py:467
  96.2 1.1 copy-done.14
  97.2 1.5 collective-permute-start.4
  100.6 19.1 %collective-permute-done.8 = bf16[2,32,16,512]{3,2,1,0:T(8,128)(2,1)} collective-permute-done((bf16[2,32,16,512]{3,2,1,0:T(8,128)(2,1)}, bf16[2,32,16,512]{3,2,1,0:T(8,128)(2,1)}, u32[]{:S(2)}, u32[]{:S(2)}) %collective-permute-start.8) | collective-permute-done | bytes 1048608 | tf_op jit(solution)/shard_map/ppermute | solution.py:467
  119.7 45.4 %conv.4 = (bf16[2,512,512]{2,1,0:T(8,128)(2,1)}, bf16[2,512,512]{2,1,0:T(8,128)(2,1)}, bf16[2,512,512]{2,1,0:T(8,128)(2,1)}, bf16[2,512,512]{2,1,0:T(8,128)(2,1)...) custom-call(s32[2]{0:T(128)} %pad_add_fusion.pos_ref, ...), custom_call_target="tpu_custom_call" | custom-call | flops 12884901888 | bytes 16777216 | tf_op jit(solution)/shard_map/conv/pallas_call | solution.py:291
  166.4 1.5 collective-permute-start.15
  168.6 45.4 %conv.5 = (bf16[2,512,512]{2,1,0:T(8,128)(2,1)}, bf16[2,512,512]{2,1,0:T(8,128)(2,1)}, bf16[2,512,512]{2,1,0:T(8,128)(2,1)}, bf16[2,512,512]{2,1,0:T(8,128)(2,1)...) custom-call(s32[2]{0:T(128)} %pad_add_fusion.pos_ref, ...), custom_call_target="tpu_custom_call", output_to_operand_aliasing={{0}: (16, {}), {1}: (17, {}), {2}: (18, {}), {3}: (19, {}),... | custom-call | flops 12884901888 | bytes 16777216 | tf_op jit(solution)/shard_map/conv/pallas_call | solution.py:291
  214.0 1.1 collective-permute-start.10
  215.0 1.6 collective-permute-start.11
  217.5 45.6 %conv.6 = (bf16[2,512,512]{2,1,0:T(8,128)(2,1)}, bf16[2,512,512]{2,1,0:T(8,128)(2,1)}, bf16[2,512,512]{2,1,0:T(8,128)(2,1)}, bf16[2,512,512]{2,1,0:T(8,128)(2,1)...) custom-call(s32[2]{0:T(128)} %pad_add_fusion.pos_ref, ...), custom_call_target="tpu_custom_call" | custom-call | flops 12884901888 | bytes 16777216 | tf_op jit(solution)/shard_map/conv/pallas_call | solution.py:291
  263.3 1.1 collective-permute-start.18
  264.4 1.2 collective-permute-start.19
  266.6 45.5 %conv.7 = (bf16[2,512,512]{2,1,0:T(8,128)(2,1)}, bf16[2,512,512]{2,1,0:T(8,128)(2,1)}, bf16[2,512,512]{2,1,0:T(8,128)(2,1)}, bf16[2,512,512]{2,1,0:T(8,128)(2,1)...) custom-call(s32[2]{0:T(128)} %pad_add_fusion.pos_ref, ...), custom_call_target="tpu_custom_call", output_to_operand_aliasing={{0}: (16, {}), {1}: (17, {}), {2}: (18, {}), {3}: (19, {}),... | custom-call | flops 12884901888 | bytes 16777216 | tf_op jit(solution)/shard_map/conv/pallas_call | solution.py:291
  313.3 1.5 collective-permute-start.23
  315.8 18.0 %smooth.1 = (bf16[16384,256]{1,0:T(8,128)(2,1)}, f32[4,32,256]{2,1,0:T(8,128)}, f32[4,32,256]{2,1,0:T(8,128)}) custom-call(s32[2]{0:T(128)} %pad_add_fusion.pos_ref, bf16[16384,256]{1,0:T(8,128)(2,1)} %bitcast.76, bf16[16384,256]{1,0:T(8,128)(2,1)} %bitcast.80, bf16[256,768]{1,0:T(8,128)(2,1)} %w_ref.9, bf16[256,256]{1,0:T(8,128)(2,1)} %constant.48.clone.pick_ref, ...), custom_call_target="tpu_custom_call" | custom-call | flops 8589934592 | bytes 33554432 | tf_op jit(solution)/shard_map/smooth/pallas_call | solution.py:649
  333.8 4.7 %collective-permute-done.22 = bf16[2,512,512]{2,1,0:T(8,128)(2,1)S(1)} collective-permute-done((bf16[2,512,512]{2,1,0:T(8,128)(2,1)}, bf16[2,512,512]{2,1,0:T(8,128)(2,1)S(1)}, u32[]{:S(2)}, u32[]{:S(2)}) %collective-permute-start.22) | collective-permute-done | bytes 1048608 | tf_op jit(solution)/shard_map/ppermute | solution.py:467
  338.4 21.9 %collective-permute-done.23 = bf16[2,512,512]{2,1,0:T(8,128)(2,1)S(1)} collective-permute-done((bf16[2,512,512]{2,1,0:T(8,128)(2,1)}, bf16[2,512,512]{2,1,0:T(8,128)(2,1)S(1)}, u32[]{:S(2)}, u32[]{:S(2)}) %collective-permute-start.23) | collective-permute-done | bytes 1048608 | tf_op jit(solution)/shard_map/ppermute | solution.py:467
  361.4 1.3 collective-permute-start.29
  362.7 1.4 collective-permute-start.30
  365.9 1.6 collective-permute-start.26
  367.5 2.3 collective-permute-start.28
  369.7 2.0 collective-permute-done.26
  372.4 4.2 collective-permute-done.27
  376.6 13.5 %back_first.1 = (f32[256,512]{1,0:T(8,128)}, bf16[192,16384]{1,0:T(8,128)(2,1)}) custom-call(s32[2]{0:T(128)} %pad_add_fusion.pos_ref, bf16[16384,256]{1,0:T(8,128)(2,1)} %bitcast.77, bf16[256,768]{1,0:T(8,128)(2,1)} %w_ref.9, bf16[256,256]{1,0:T(8,128)(2,1)} %constant.48.clone.pick_ref, bf16[2,32,16,512]{3,2,1,0:T(8,128)(2,1)} %bitcast.104, ...), custom_call_target="tpu_custom_call" | custom-call | flops 6442450944 | bytes 25165824 | tf_op jit(solution)/shard_map/back_first/pallas_call | solution.py:670
  390.1 19.4 %collective-permute-done.30 = bf16[2,512,512]{2,1,0:T(8,128)(2,1)S(1)} collective-permute-done((bf16[2,512,512]{2,1,0:T(8,128)(2,1)}, bf16[2,512,512]{2,1,0:T(8,128)(2,1)S(1)}, u32[]{:S(2)}, u32[]{:S(2)}) %collective-permute-start.30) | collective-permute-done | bytes 1048608 | tf_op jit(solution)/shard_map/ppermute | solution.py:467
  409.5 1.6 collective-permute-done.31
  411.1 1.1 copy-done.4
  412.2 8.3 %back_last.1 = (f32[4,32,512]{2,1,0:T(8,128)}, f32[4,32,512]{2,1,0:T(8,128)}) custom-call(s32[2]{0:T(128)} %pad_add_fusion.pos_ref, bf16[16384,256]{1,0:T(8,128)(2,1)} %bitcast.78, bf16[192,16384]{1,0:T(8,128)(2,1)} %get-tuple-element.267.feat_ref, f32[256,512]{1,0:T(8,128)} %get-tuple-element.268.earlier_ref, bf16[2,32,16,512]{3,2,1,0:T(8,128)(2,1)} %bitcast.84, ...), custom_call_target="tpu_custom_call" | custom-call | flops 2147483648 | bytes 20971520 | tf_op jit(solution)/shard_map/back_last/pallas_call | solution.py:688
  420.5 1.7 collective-permute-done.32
  423.3 1.6 collective-permute-start.33
  424.9 2.3 collective-permute-start.35
  427.9 1.6 collective-permute-done.33
  430.1 3.4 collective-permute-done.34
  434.5 1.4 collective-permute-start.38
  435.9 1.2 collective-permute-start.36
  437.1 2.5 collective-permute-done.37
  439.7 1.3 collective-permute-done.38
  441.7 1.3 collective-permute-done.39
  (96 shorter events, 18.3 us)
Async XLA Ops:
  7.2 112.6 %all-gather.3.cloned.1.call-start = ((), (), s32[]{:S(2)}) async-start(), calls=%async_computation.1 | async-start | bytes 2621440 | tf_op jit(solution)/shard_map/all_gather | solution.py:623
  14.5 56.0 %collective-permute-start = (bf16[2,32,16,512]{3,2,1,0:T(8,128)(2,1)}, bf16[2,32,16,512]{3,2,1,0:T(8,128)(2,1)S(1)}, u32[]{:S(2)}, u32[]{:S(2)}) collective-permute-start(bf16[2,32,16,512]{3,2,1,0:T(8,128)(2,1)} %get-tuple-element.150), channel_id=1, source_target_pairs={{0,2},{1,3},{2,0},{3,1},{4,6},{5,7},{6,4},{7,5},{8,10},{9,11},{10,... | collective-permute-start | bytes 3145736 | tf_op jit(solution)/shard_map/ppermute | solution.py:467
  17.4 53.0 %collective-permute-start.1 = (bf16[2,32,16,512]{3,2,1,0:T(8,128)(2,1)}, bf16[2,32,16,512]{3,2,1,0:T(8,128)(2,1)}, u32[]{:S(2)}, u32[]{:S(2)}) collective-permute-start(bf16[2,32,16,512]{3,2,1,0:T(8,128)(2,1)} %get-tuple-element.151), channel_id=1, source_target_pairs={{0,4},{1,5},{2,6},{3,7},{4,0},{5,1},{6,2},{7,3},{8,12},{9,13},{10,... | collective-permute-start | bytes 3145736 | tf_op jit(solution)/shard_map/ppermute | solution.py:467
  19.0 51.5 %collective-permute-start.2 = (bf16[2,32,16,512]{3,2,1,0:T(8,128)(2,1)}, bf16[2,32,16,512]{3,2,1,0:T(8,128)(2,1)}, u32[]{:S(2)}, u32[]{:S(2)}) collective-permute-start(bf16[2,32,16,512]{3,2,1,0:T(8,128)(2,1)} %get-tuple-element.152), channel_id=1, source_target_pairs={{0,6},{1,7},{2,4},{3,5},{4,2},{5,3},{6,0},{7,1},{8,14},{9,15},{10,... | collective-permute-start | bytes 3145736 | tf_op jit(solution)/shard_map/ppermute | solution.py:467
  70.5 25.7 %collective-permute-start.7 = (bf16[2,32,16,512]{3,2,1,0:T(8,128)(2,1)}, bf16[2,32,16,512]{3,2,1,0:T(8,128)(2,1)S(1)}, u32[]{:S(2)}, u32[]{:S(2)}) collective-permute-start(bf16[2,32,16,512]{3,2,1,0:T(8,128)(2,1)} %get-tuple-element.165), channel_id=1, source_target_pairs={{0,3},{1,2},{2,1},{3,0},{4,7},{5,6},{6,5},{7,4},{8,11},{9,10},{10,... | collective-permute-start | bytes 3145736 | tf_op jit(solution)/shard_map/ppermute | solution.py:467
  70.6 28.1 %collective-permute-start.6 = (bf16[2,32,16,512]{3,2,1,0:T(8,128)(2,1)}, bf16[2,32,16,512]{3,2,1,0:T(8,128)(2,1)S(1)}, u32[]{:S(2)}, u32[]{:S(2)}) collective-permute-start(bf16[2,32,16,512]{3,2,1,0:T(8,128)(2,1)} %get-tuple-element.163), channel_id=1, source_target_pairs={{0,1},{1,0},{2,3},{3,2},{4,5},{5,4},{6,7},{7,6},{8,9},{9,8},{10,11... | collective-permute-start | bytes 3145736 | tf_op jit(solution)/shard_map/ppermute | solution.py:467
  71.6 48.0 %collective-permute-start.8 = (bf16[2,32,16,512]{3,2,1,0:T(8,128)(2,1)}, bf16[2,32,16,512]{3,2,1,0:T(8,128)(2,1)}, u32[]{:S(2)}, u32[]{:S(2)}) collective-permute-start(bf16[2,32,16,512]{3,2,1,0:T(8,128)(2,1)} %get-tuple-element.167), channel_id=1, source_target_pairs={{0,5},{1,4},{2,7},{3,6},{4,1},{5,0},{6,3},{7,2},{8,13},{9,12},{10,... | collective-permute-start | bytes 3145736 | tf_op jit(solution)/shard_map/ppermute | solution.py:467
  72.3 47.4 %collective-permute-start.9 = (bf16[2,32,16,512]{3,2,1,0:T(8,128)(2,1)}, bf16[2,32,16,512]{3,2,1,0:T(8,128)(2,1)}, u32[]{:S(2)}, u32[]{:S(2)}) collective-permute-start(bf16[2,32,16,512]{3,2,1,0:T(8,128)(2,1)} %get-tuple-element.169), channel_id=1, source_target_pairs={{0,7},{1,6},{2,5},{3,4},{4,3},{5,2},{6,1},{7,0},{8,15},{9,14},{10,... | collective-permute-start | bytes 3145736 | tf_op jit(solution)/shard_map/ppermute | solution.py:467
  85.6 79.5 %collective-permute-start.3 = (bf16[2,512,512]{2,1,0:T(8,128)(2,1)}, bf16[2,512,512]{2,1,0:T(8,128)(2,1)S(1)}, u32[]{:S(2)}, u32[]{:S(2)}) collective-permute-start(bf16[2,512,512]{2,1,0:T(8,128)(2,1)} %bitcast.113), channel_id=1, source_target_pairs={{0,2},{1,3},{2,0},{3,1},{4,6},{5,7},{6,4},{7,5},{8,10},{9,11},{10,... | collective-permute-start | bytes 3145736 | tf_op jit(solution)/shard_map/ppermute | solution.py:467
  97.2 67.9 %collective-permute-start.4 = (bf16[2,512,512]{2,1,0:T(8,128)(2,1)}, bf16[2,512,512]{2,1,0:T(8,128)(2,1)S(1)}, u32[]{:S(2)}, u32[]{:S(2)}) collective-permute-start(bf16[2,512,512]{2,1,0:T(8,128)(2,1)} %bitcast.112), channel_id=1, source_target_pairs={{0,4},{1,5},{2,6},{3,7},{4,0},{5,1},{6,2},{7,3},{8,12},{9,13},{10,... | collective-permute-start | bytes 3145736 | tf_op jit(solution)/shard_map/ppermute | solution.py:467
  99.7 65.5 %collective-permute-start.5 = (bf16[2,512,512]{2,1,0:T(8,128)(2,1)}, bf16[2,512,512]{2,1,0:T(8,128)(2,1)S(1)}, u32[]{:S(2)}, u32[]{:S(2)}) collective-permute-start(bf16[2,512,512]{2,1,0:T(8,128)(2,1)} %bitcast.111), channel_id=1, source_target_pairs={{0,6},{1,7},{2,4},{3,5},{4,2},{5,3},{6,0},{7,1},{8,14},{9,15},{10,... | collective-permute-start | bytes 3145736 | tf_op jit(solution)/shard_map/ppermute | solution.py:467
  165.1 48.8 %copy-start.5 = (bf16[2,512,512]{2,1,0:T(8,128)(2,1)}, bf16[2,512,512]{2,1,0:T(8,128)(2,1)S(1)}, u32[]{:S(2)}) copy-start(bf16[2,512,512]{2,1,0:T(8,128)(2,1)S(1)} %collective-permute-done.3.args_2_) | copy-start | bytes 3145732
  165.2 48.8 %copy-start.6 = (bf16[2,512,512]{2,1,0:T(8,128)(2,1)}, bf16[2,512,512]{2,1,0:T(8,128)(2,1)S(1)}, u32[]{:S(2)}) copy-start(bf16[2,512,512]{2,1,0:T(8,128)(2,1)S(1)} %collective-permute-done.4.args_4_) | copy-start | bytes 3145732
  165.2 48.8 %copy-start.7 = (bf16[2,512,512]{2,1,0:T(8,128)(2,1)}, bf16[2,512,512]{2,1,0:T(8,128)(2,1)S(1)}, u32[]{:S(2)}) copy-start(bf16[2,512,512]{2,1,0:T(8,128)(2,1)S(1)} %collective-permute-done.5.args_6_) | copy-start | bytes 3145732
  165.2 49.9 %collective-permute-start.13 = (bf16[2,512,512]{2,1,0:T(8,128)(2,1)}, bf16[2,512,512]{2,1,0:T(8,128)(2,1)}, u32[]{:S(2)}, u32[]{:S(2)}) collective-permute-start(bf16[2,512,512]{2,1,0:T(8,128)(2,1)} %bitcast.107), channel_id=1, source_target_pairs={{0,1},{1,0},{2,3},{3,2},{4,5},{5,4},{6,7},{7,6},{8,9},{9,8},{10,11... | collective-permute-start | bytes 3145736 | tf_op jit(solution)/shard_map/ppermute | solution.py:467
  165.6 51.0 %collective-permute-start.14 = (bf16[2,512,512]{2,1,0:T(8,128)(2,1)}, bf16[2,512,512]{2,1,0:T(8,128)(2,1)}, u32[]{:S(2)}, u32[]{:S(2)}) collective-permute-start(bf16[2,512,512]{2,1,0:T(8,128)(2,1)} %bitcast.103), channel_id=1, source_target_pairs={{0,3},{1,2},{2,1},{3,0},{4,7},{5,6},{6,5},{7,4},{8,11},{9,10},{10,... | collective-permute-start | bytes 3145736 | tf_op jit(solution)/shard_map/ppermute | solution.py:467
  166.4 51.1 %collective-permute-start.15 = (bf16[2,512,512]{2,1,0:T(8,128)(2,1)}, bf16[2,512,512]{2,1,0:T(8,128)(2,1)}, u32[]{:S(2)}, u32[]{:S(2)}) collective-permute-start(bf16[2,512,512]{2,1,0:T(8,128)(2,1)} %bitcast.100), channel_id=1, source_target_pairs={{0,5},{1,4},{2,7},{3,6},{4,1},{5,0},{6,3},{7,2},{8,13},{9,12},{10,... | collective-permute-start | bytes 3145736 | tf_op jit(solution)/shard_map/ppermute | solution.py:467
  167.9 49.6 %collective-permute-start.16 = (bf16[2,512,512]{2,1,0:T(8,128)(2,1)}, bf16[2,512,512]{2,1,0:T(8,128)(2,1)}, u32[]{:S(2)}, u32[]{:S(2)}) collective-permute-start(bf16[2,512,512]{2,1,0:T(8,128)(2,1)} %bitcast.99), channel_id=1, source_target_pairs={{0,7},{1,6},{2,5},{3,4},{4,3},{5,2},{6,1},{7,0},{8,15},{9,14},{10,... | collective-permute-start | bytes 3145736 | tf_op jit(solution)/shard_map/ppermute | solution.py:467
  214.0 49.2 %collective-permute-start.10 = (bf16[2,512,512]{2,1,0:T(8,128)(2,1)}, bf16[2,512,512]{2,1,0:T(8,128)(2,1)S(1)}, u32[]{:S(2)}, u32[]{:S(2)}) collective-permute-start(bf16[2,512,512]{2,1,0:T(8,128)(2,1)} %get-tuple-element.198), channel_id=1, source_target_pairs={{0,2},{1,3},{2,0},{3,1},{4,6},{5,7},{6,4},{7,5},{8,10},{9,11},{10,... | collective-permute-start | bytes 3145736 | tf_op jit(solution)/shard_map/ppermute | solution.py:467
  215.0 48.1 %collective-permute-start.11 = (bf16[2,512,512]{2,1,0:T(8,128)(2,1)}, bf16[2,512,512]{2,1,0:T(8,128)(2,1)S(1)}, u32[]{:S(2)}, u32[]{:S(2)}) collective-permute-start(bf16[2,512,512]{2,1,0:T(8,128)(2,1)} %get-tuple-element.200), channel_id=1, source_target_pairs={{0,4},{1,5},{2,6},{3,7},{4,0},{5,1},{6,2},{7,3},{8,12},{9,13},{10,... | collective-permute-start | bytes 3145736 | tf_op jit(solution)/shard_map/ppermute | solution.py:467
  216.6 46.6 %collective-permute-start.12 = (bf16[2,512,512]{2,1,0:T(8,128)(2,1)}, bf16[2,512,512]{2,1,0:T(8,128)(2,1)S(1)}, u32[]{:S(2)}, u32[]{:S(2)}) collective-permute-start(bf16[2,512,512]{2,1,0:T(8,128)(2,1)} %get-tuple-element.202), channel_id=1, source_target_pairs={{0,6},{1,7},{2,4},{3,5},{4,2},{5,3},{6,0},{7,1},{8,14},{9,15},{10,... | collective-permute-start | bytes 3145736 | tf_op jit(solution)/shard_map/ppermute | solution.py:467
  263.2 48.9 %copy-start.9 = (bf16[2,512,512]{2,1,0:T(8,128)(2,1)}, bf16[2,512,512]{2,1,0:T(8,128)(2,1)S(1)}, u32[]{:S(2)}) copy-start(bf16[2,512,512]{2,1,0:T(8,128)(2,1)S(1)} %collective-permute-done.10) | copy-start | bytes 3145732
  263.2 48.9 %copy-start.10 = (bf16[2,512,512]{2,1,0:T(8,128)(2,1)}, bf16[2,512,512]{2,1,0:T(8,128)(2,1)S(1)}, u32[]{:S(2)}) copy-start(bf16[2,512,512]{2,1,0:T(8,128)(2,1)S(1)} %collective-permute-done.11) | copy-start | bytes 3145732
  263.2 48.9 %copy-start.11 = (bf16[2,512,512]{2,1,0:T(8,128)(2,1)}, bf16[2,512,512]{2,1,0:T(8,128)(2,1)S(1)}, u32[]{:S(2)}) copy-start(bf16[2,512,512]{2,1,0:T(8,128)(2,1)S(1)} %collective-permute-done.12) | copy-start | bytes 3145732
  263.2 49.0 %collective-permute-start.17 = (bf16[2,512,512]{2,1,0:T(8,128)(2,1)}, bf16[2,512,512]{2,1,0:T(8,128)(2,1)}, u32[]{:S(2)}, u32[]{:S(2)}) collective-permute-start(bf16[2,512,512]{2,1,0:T(8,128)(2,1)} %get-tuple-element.240), channel_id=1, source_target_pairs={{0,1},{1,0},{2,3},{3,2},{4,5},{5,4},{6,7},{7,6},{8,9},{9,8},{10,11... | collective-permute-start | bytes 3145736 | tf_op jit(solution)/shard_map/ppermute | solution.py:467
  263.3 50.0 %collective-permute-start.18 = (bf16[2,512,512]{2,1,0:T(8,128)(2,1)}, bf16[2,512,512]{2,1,0:T(8,128)(2,1)}, u32[]{:S(2)}, u32[]{:S(2)}) collective-permute-start(bf16[2,512,512]{2,1,0:T(8,128)(2,1)} %get-tuple-element.242), channel_id=1, source_target_pairs={{0,3},{1,2},{2,1},{3,0},{4,7},{5,6},{6,5},{7,4},{8,11},{9,10},{10,... | collective-permute-start | bytes 3145736 | tf_op jit(solution)/shard_map/ppermute | solution.py:467
  264.4 50.4 %collective-permute-start.19 = (bf16[2,512,512]{2,1,0:T(8,128)(2,1)}, bf16[2,512,512]{2,1,0:T(8,128)(2,1)}, u32[]{:S(2)}, u32[]{:S(2)}) collective-permute-start(bf16[2,512,512]{2,1,0:T(8,128)(2,1)} %get-tuple-element.244), channel_id=1, source_target_pairs={{0,5},{1,4},{2,7},{3,6},{4,1},{5,0},{6,3},{7,2},{8,13},{9,12},{10,... | collective-permute-start | bytes 3145736 | tf_op jit(solution)/shard_map/ppermute | solution.py:467
  265.6 50.1 %collective-permute-start.20 = (bf16[2,512,512]{2,1,0:T(8,128)(2,1)}, bf16[2,512,512]{2,1,0:T(8,128)(2,1)}, u32[]{:S(2)}, u32[]{:S(2)}) collective-permute-start(bf16[2,512,512]{2,1,0:T(8,128)(2,1)} %get-tuple-element.246), channel_id=1, source_target_pairs={{0,7},{1,6},{2,5},{3,4},{4,3},{5,2},{6,1},{7,0},{8,15},{9,14},{10,... | collective-permute-start | bytes 3145736 | tf_op jit(solution)/shard_map/ppermute | solution.py:467
  312.1 21.6 %collective-permute-start.21 = (bf16[2,512,512]{2,1,0:T(8,128)(2,1)}, bf16[2,512,512]{2,1,0:T(8,128)(2,1)S(1)}, u32[]{:S(2)}, u32[]{:S(2)}) collective-permute-start(bf16[2,512,512]{2,1,0:T(8,128)(2,1)} %get-tuple-element.249), channel_id=1, source_target_pairs={{0,1},{1,0},{2,3},{3,2},{4,5},{5,4},{6,7},{7,6},{8,9},{9,8},{10,11... | collective-permute-start | bytes 3145736 | tf_op jit(solution)/shard_map/ppermute | solution.py:467
  312.2 26.2 %collective-permute-start.22 = (bf16[2,512,512]{2,1,0:T(8,128)(2,1)}, bf16[2,512,512]{2,1,0:T(8,128)(2,1)S(1)}, u32[]{:S(2)}, u32[]{:S(2)}) collective-permute-start(bf16[2,512,512]{2,1,0:T(8,128)(2,1)} %get-tuple-element.250), channel_id=1, source_target_pairs={{0,2},{1,3},{2,0},{3,1},{4,6},{5,7},{6,4},{7,5},{8,10},{9,11},{10,... | collective-permute-start | bytes 3145736 | tf_op jit(solution)/shard_map/ppermute | solution.py:467
  313.3 47.1 %collective-permute-start.23 = (bf16[2,512,512]{2,1,0:T(8,128)(2,1)}, bf16[2,512,512]{2,1,0:T(8,128)(2,1)S(1)}, u32[]{:S(2)}, u32[]{:S(2)}) collective-permute-start(bf16[2,512,512]{2,1,0:T(8,128)(2,1)} %get-tuple-element.252), channel_id=1, source_target_pairs={{0,4},{1,5},{2,6},{3,7},{4,0},{5,1},{6,2},{7,3},{8,12},{9,13},{10,... | collective-permute-start | bytes 3145736 | tf_op jit(solution)/shard_map/ppermute | solution.py:467
  314.8 46.5 %collective-permute-start.24 = (bf16[2,512,512]{2,1,0:T(8,128)(2,1)}, bf16[2,512,512]{2,1,0:T(8,128)(2,1)}, u32[]{:S(2)}, u32[]{:S(2)}) collective-permute-start(bf16[2,512,512]{2,1,0:T(8,128)(2,1)} %get-tuple-element.254), channel_id=1, source_target_pairs={{0,6},{1,7},{2,4},{3,5},{4,2},{5,3},{6,0},{7,1},{8,14},{9,15},{10,... | collective-permute-start | bytes 3145736 | tf_op jit(solution)/shard_map/ppermute | solution.py:467
  333.8 27.5 %copy-start.12 = (bf16[2,512,512]{2,1,0:T(8,128)(2,1)}, bf16[2,512,512]{2,1,0:T(8,128)(2,1)S(1)}, u32[]{:S(2)}) copy-start(bf16[2,512,512]{2,1,0:T(8,128)(2,1)S(1)} %collective-permute-done.21) | copy-start | bytes 3145732
  361.3 3.6 collective-permute-start.25
  361.4 28.7 %collective-permute-start.29 = (bf16[2,512,512]{2,1,0:T(8,128)(2,1)}, bf16[2,512,512]{2,1,0:T(8,128)(2,1)S(1)}, u32[]{:S(2)}, u32[]{:S(2)}) collective-permute-start(bf16[2,512,512]{2,1,0:T(8,128)(2,1)} %get-tuple-element.269), channel_id=1, source_target_pairs={{0,3},{1,2},{2,1},{3,0},{4,7},{5,6},{6,5},{7,4},{8,11},{9,10},{10,... | collective-permute-start | bytes 3145736 | tf_op jit(solution)/shard_map/ppermute | solution.py:467
  362.7 46.8 %collective-permute-start.30 = (bf16[2,512,512]{2,1,0:T(8,128)(2,1)}, bf16[2,512,512]{2,1,0:T(8,128)(2,1)S(1)}, u32[]{:S(2)}, u32[]{:S(2)}) collective-permute-start(bf16[2,512,512]{2,1,0:T(8,128)(2,1)} %get-tuple-element.270), channel_id=1, source_target_pairs={{0,5},{1,4},{2,7},{3,6},{4,1},{5,0},{6,3},{7,2},{8,13},{9,12},{10,... | collective-permute-start | bytes 3145736 | tf_op jit(solution)/shard_map/ppermute | solution.py:467
  364.1 47.0 %collective-permute-start.31 = (bf16[2,512,512]{2,1,0:T(8,128)(2,1)}, bf16[2,512,512]{2,1,0:T(8,128)(2,1)S(1)}, u32[]{:S(2)}, u32[]{:S(2)}) collective-permute-start(bf16[2,512,512]{2,1,0:T(8,128)(2,1)} %get-tuple-element.271), channel_id=1, source_target_pairs={{0,7},{1,6},{2,5},{3,4},{4,3},{5,2},{6,1},{7,0},{8,15},{9,14},{10,... | collective-permute-start | bytes 3145736 | tf_op jit(solution)/shard_map/ppermute | solution.py:467
  365.9 5.9 %collective-permute-start.26 = (f32[32,256]{1,0:T(8,128)S(1)}, f32[32,256]{1,0:T(8,128)S(1)}, u32[]{:S(2)}, u32[]{:S(2)}) collective-permute-start(f32[32,256]{1,0:T(8,128)S(1)} %get-tuple-element.279), channel_id=1, source_target_pairs={{0,8},{8,16},{16,24},{24,0},{1,9},{9,17},{17,25},{25,1},{2,10},{10... | collective-permute-start | bytes 98312 | tf_op jit(solution)/shard_map/ppermute | solution.py:528
  367.5 5.0 %collective-permute-start.28 = (f32[32,256]{1,0:T(8,128)S(1)}, f32[32,256]{1,0:T(8,128)S(1)}, u32[]{:S(2)}, u32[]{:S(2)}) collective-permute-start(f32[32,256]{1,0:T(8,128)S(1)} %get-tuple-element.280), channel_id=1, source_target_pairs={{0,24},{8,0},{16,8},{24,16},{1,25},{9,1},{17,9},{25,17},{2,26},{10... | collective-permute-start | bytes 98312 | tf_op jit(solution)/shard_map/ppermute | solution.py:528
  371.8 4.8 %collective-permute-start.27 = (f32[32,256]{1,0:T(8,128)S(1)}, f32[32,256]{1,0:T(8,128)S(1)}, u32[]{:S(2)}, u32[]{:S(2)}) collective-permute-start(f32[32,256]{1,0:T(8,128)S(1)} %get-tuple-element.281), channel_id=1, source_target_pairs={{0,16},{8,24},{16,0},{24,8},{1,17},{9,25},{17,1},{25,9},{2,18},{10... | collective-permute-start | bytes 98312 | tf_op jit(solution)/shard_map/ppermute | solution.py:528
  420.5 1.8 collective-permute-start.32
  423.3 6.2 %collective-permute-start.33 = (f32[32,512]{1,0:T(8,128)S(1)}, f32[32,512]{1,0:T(8,128)S(1)}, u32[]{:S(2)}, u32[]{:S(2)}) collective-permute-start(f32[32,512]{1,0:T(8,128)S(1)} %get-tuple-element.274), channel_id=1, source_target_pairs={{0,8},{8,16},{16,24},{24,0},{1,9},{9,17},{17,25},{25,1},{2,10},{10... | collective-permute-start | bytes 196616 | tf_op jit(solution)/shard_map/ppermute | solution.py:528
  424.9 5.3 %collective-permute-start.35 = (f32[32,512]{1,0:T(8,128)S(1)}, f32[32,512]{1,0:T(8,128)S(1)}, u32[]{:S(2)}, u32[]{:S(2)}) collective-permute-start(f32[32,512]{1,0:T(8,128)S(1)} %get-tuple-element.275), channel_id=1, source_target_pairs={{0,24},{8,0},{16,8},{24,16},{1,25},{9,1},{17,9},{25,17},{2,26},{10... | collective-permute-start | bytes 196616 | tf_op jit(solution)/shard_map/ppermute | solution.py:528
  427.1 6.4 %collective-permute-start.34 = (f32[32,512]{1,0:T(8,128)S(1)}, f32[32,512]{1,0:T(8,128)S(1)}, u32[]{:S(2)}, u32[]{:S(2)}) collective-permute-start(f32[32,512]{1,0:T(8,128)S(1)} %get-tuple-element.276), channel_id=1, source_target_pairs={{0,16},{8,24},{16,0},{24,8},{1,17},{9,25},{17,1},{25,9},{2,18},{10... | collective-permute-start | bytes 196616 | tf_op jit(solution)/shard_map/ppermute | solution.py:528
  433.6 6.1 %collective-permute-start.37 = (f32[32,768]{1,0:T(8,128)S(1)}, f32[32,768]{1,0:T(8,128)S(1)}, u32[]{:S(2)}, u32[]{:S(2)}) collective-permute-start(f32[32,768]{1,0:T(8,128)S(1)} %pad_maximum_fusion.1), channel_id=1, source_target_pairs={{0,4},{1,5},{2,6},{3,7},{4,0},{5,1},{6,2},{7,3},{8,12},{9,13},{10,... | collective-permute-start | bytes 294920 | tf_op jit(solution)/shard_map/ppermute | solution.py:519
  434.5 6.4 %collective-permute-start.38 = (f32[32,768]{1,0:T(8,128)S(1)}, f32[32,768]{1,0:T(8,128)S(1)}, u32[]{:S(2)}, u32[]{:S(2)}) collective-permute-start(f32[32,768]{1,0:T(8,128)S(1)} %pad_maximum_fusion.1), channel_id=1, source_target_pairs={{0,6},{1,7},{2,4},{3,5},{4,2},{5,3},{6,0},{7,1},{8,14},{9,15},{10,... | collective-permute-start | bytes 294920 | tf_op jit(solution)/shard_map/ppermute | solution.py:519
  435.9 5.7 %collective-permute-start.36 = (f32[32,768]{1,0:T(8,128)S(1)}, f32[32,768]{1,0:T(8,128)S(1)}, u32[]{:S(2)}, u32[]{:S(2)}) collective-permute-start(f32[32,768]{1,0:T(8,128)S(1)} %pad_maximum_fusion.1), channel_id=1, source_target_pairs={{0,2},{1,3},{2,0},{3,1},{4,6},{5,7},{6,4},{7,5},{8,10},{9,11},{10,... | collective-permute-start | bytes 294920 | tf_op jit(solution)/shard_map/ppermute | solution.py:519
  441.6 1.4 collective-permute-start.39
  (10 other events, 98.5 us)
Sparse Core Ops, SparseCore 0:
  70.6 46.2 all-gather.2
